TPU v7x, 128 devices: a whole 4x4x4 slice. The times are simulated.
128 devices in a mesh: rows: 8 (over y, z_lo), frames: 16 (over z_hi, x, core).
Axes of the slice: x: 4, y: 4, z: 4 (z_hi: 2, z_lo: 2; z = z_hi * 2 + z_lo), core: 2. Of those that a mesh axis runs over, the one named last changes fastest.
Arguments:
- latents: bfloat16 [16384, 128], P(('rows', 'frames')), may hold values from -6 to 6
- tile_slot: int32 [16384], P(('rows', 'frames')), may hold values from 0 to 16383, as said below
- w_in: bfloat16 [3, 3, 3, 16, 384], replicated, may hold values from -0.3125 to 0.3125
- b_in: float32 [384], replicated, may hold values from -3 to 3
- gain_in: float32 [384], replicated, may hold values from 0.1 to 1.9
- w_time: bfloat16 [3, 384, 768], replicated, may hold values from -0.1875 to 0.1875
- b_time: float32 [768], replicated, may hold values from -3 to 3
- w_lift: bfloat16 [3, 3, 384, 192], replicated, may hold values from -0.109375 to 0.109375
- b_lift: float32 [192], replicated, may hold values from -3 to 3
- gain_lift: float32 [192], replicated, may hold values from 0.1 to 1.9
- w_final: bfloat16 [3, 3, 192, 96], replicated, may hold values from -0.15625 to 0.15625
- b_final: float32 [96], replicated, may hold values from -3 to 3
Outputs:
- decoded: bfloat16 [64, 128, 49152], P('frames', 'rows')
Inputs may be any that keep to these rules, and one draw needn't show every extreme that they name: tile_slot is a permutation of the 16384 canvas slots. Of the 128 tiles that one device holds, at most 2 have slots in the block of one owner (slot // 128), and in every draw each device has exactly 2 for some owner.
All inputs are finite; a program needn't handle non-finite values.
Results may differ from a plain program's by a relative error of at most 0.0055.
Values may be sent and summed in bfloat16 or wider, within the bound.
A program may use at most 128 MiB of HBM per device.

v0:
```python
import functools

import jax
import jax.numpy as jnp
from jax import lax
from jax.experimental import pallas as pl
from jax.experimental.pallas import tpu as pltpu
from jax.sharding import PartitionSpec as P

BF16, F32 = jnp.bfloat16, jnp.float32
XB = 16
SC = 4


def silu(n):
    half = 0.5 * n
    return half + half * jnp.tanh(half)


def pick(parts, tap, phase):
    if phase == 0:
        return parts[0] + parts[1] if tap == 0 else parts[2]
    return parts[0] if tap == 0 else parts[1] + parts[2]


def summed_taps(load, ty, tx, py, px):
    rows = [pick([load(dy, dx) for dy in range(3)], ty, py) for dx in range(3)]
    return pick(rows, tx, px)


def weights_kernel(win_ref, wlift_ref, wfinal_ref, band_ref, lift_ref, final_ref):
    channels = win_ref.shape[-1]
    band_ref[...] = jnp.zeros_like(band_ref)
    for k in range(3):
        for dy in range(3):
            for dx in range(3):
                taps = win_ref[k, dy, dx]
                for pp in range(2):
                    row = 256 * k + 64 * dy + 16 * (dx + pp)
                    band_ref[row : row + 16, channels * pp : channels * (pp + 1)] = taps
    depth = wlift_ref.shape[2]

    def lift_rows(step, carry):
        row = pl.multiple_of(step * 64, 64)

        def wide(dy, dx):
            return wlift_ref[dy, dx, pl.ds(row, 64), 0:128].astype(F32)

        def narrow(dy, dx):
            return wlift_ref[dy, dx, pl.ds(row, 64), 128:192].astype(F32)

        for ty in range(2):
            for tx in range(2):
                for px in range(2):
                    tiles = [
                        summed_taps(wide, ty, tx, 0, px),
                        jnp.concatenate([summed_taps(narrow, ty, tx, py, px) for py in range(2)], axis=-1),
                        summed_taps(wide, ty, tx, 1, px),
                    ]
                    for n, tile in enumerate(tiles):
                        lane = 384 * px + 128 * n
                        lift_ref[pl.ds(depth * (2 * ty + tx) + row, 64), lane : lane + 128] = tile.astype(BF16)
        return carry

    lax.fori_loop(0, depth // 64, lift_rows, 0)

    def final_rows(part):
        rows = slice(64 * part, 64 * (part + 1))
        low = lax.broadcasted_iota(jnp.int32, (64, 128), 1) < 64
        pad = jnp.zeros((64, 32), F32)

        def load(dy, dx):
            return wfinal_ref[dy, dx, rows, :].astype(F32)

        for ty in range(2):
            for tx in range(2):
                for qy in range(2):
                    q0, q1 = (
                        jnp.concatenate([summed_taps(load, ty, tx, qy, qx), pad], axis=-1) for qx in range(2)
                    )
                    r0, r1 = pltpu.roll(q0, 96, 1), pltpu.roll(q1, 64, 1)
                    pairs = (
                        (jnp.where(low, r1, r0), jnp.where(low, r0, r1)),
                        (pltpu.roll(q0, 32, 1), q1),
                    )
                    for xpar, tiles in enumerate(pairs):
                        px = tx if xpar else 1 - tx
                        for jpar in range(2):
                            py = ty if jpar else 1 - ty
                            slot = 384 * px
                            if part < 2:
                                slot += 256 * py + 64 * part
                            else:
                                slot += 128 + 64 * py
                            for n, tile in enumerate(tiles):
                                lane = 256 * qy + 128 * n
                                final_ref[2 * jpar + xpar, slot : slot + 64, lane : lane + 128] = tile.astype(BF16)

    for part in range(3):
        final_rows(part)


def make_weights(w_in, w_lift, w_final):
    whole = pl.BlockSpec(memory_space=pltpu.VMEM)
    return pl.pallas_call(
        weights_kernel,
        in_specs=[whole] * 3,
        out_specs=[whole] * 3,
        out_shape=[
            jax.ShapeDtypeStruct((768, 768), BF16),
            jax.ShapeDtypeStruct((1536, 768), BF16),
            jax.ShapeDtypeStruct((4, 768, 512), BF16),
        ],
        compiler_params=pltpu.CompilerParams(vmem_limit_bytes=48 * 1024 * 1024),
        name="weights",
    )(w_in, w_lift, w_final)


def front(place_ref, blocks_ref, band_ref, bin_ref, gin_ref, wtime_ref, btime_ref, grid_ref, dbl_ref):
    row, frame = place_ref[0], place_ref[1]
    top, bottom = row == 0, row == place_ref[2] - 1
    out_row = lax.broadcasted_iota(jnp.int32, (256, 384), 0)
    in_row = lax.broadcasted_iota(jnp.int32, (256, 384), 1)
    y_in = out_row % 8 + 2
    wanted = (y_in // 4) * 128 + (out_row // 128) * 64 + (y_in % 4) * 16 + (out_row // 8) % 16
    inside = jnp.logical_and(
        jnp.logical_or(jnp.logical_not(top), y_in >= 4), jnp.logical_or(jnp.logical_not(bottom), y_in < 8)
    )
    chosen = jnp.logical_and(in_row == wanted, inside)
    zero_col = jnp.zeros((6, 1, 8, 128), F32)
    grid_ref[:, 0:1] = zero_col
    grid_ref[:, 17:18] = zero_col
    for part in range(3):
        select = jnp.where(jnp.logical_and(chosen, frame + part >= 2), 1.0, 0.0).astype(BF16)
        cells = blocks_ref[part].reshape(384, 128)
        picked = jnp.dot(select, cells, preferred_element_type=F32)
        grid_ref[2 * part : 2 * part + 2, 1:17] = picked.reshape(2, 16, 8, 128)

    lane = lax.broadcasted_iota(jnp.int32, (1, 1, 1, 128), 3)
    sub = lax.broadcasted_iota(jnp.int32, (1, 1, 8, 1), 2)
    edge_col = jnp.zeros((1, 16, 384), BF16)
    for v in range(3):
        dbl_ref[v, 0:1] = edge_col
        dbl_ref[v, dbl_ref.shape[1] - 1 :] = edge_col

    def chunk(step, carry):
        s0 = step * SC
        cells = grid_ref[:, pl.ds(s0, SC + 2)]
        flat = cells.reshape(6 * (SC + 2), 8, 128)
        turned = [pltpu.roll(flat, 1, 1), flat, pltpu.roll(flat, 7, 1)]
        pieces = []
        for q in range(4):
            shift = (16 - 32 * q) % 128
            parts = []
            for d, lanes in enumerate((shift, shift + 64, shift)):
                moved = pltpu.roll(turned[d], lanes % 128, 2).reshape(6, SC + 2, 8, 128)
                own = moved[:, 1:-1]
                at = 64 * (d % 2)
                if q == 0:
                    own = jnp.where((lane >= at) & (lane < at + 16), moved[:, :-2], own)
                if q == 3:
                    own = jnp.where((lane >= at + 48) & (lane < at + 64), moved[:, 2:], own)
                parts.append(own)
            first = jnp.where(lane < 64, parts[0], parts[1])
            pieces.append(jnp.concatenate([first, parts[2]], axis=-1))
        patch = jnp.stack(pieces, axis=2).reshape(6, SC * 4 * 8, 256).astype(BF16)
        patch = jnp.concatenate([patch[k : k + 4] for k in range(3)], axis=-1)
        hidden = jnp.dot(patch.reshape(4 * SC * 32, 768), band_ref[...], preferred_element_type=F32)
        halves = []
        for pp in range(2):
            h = hidden[:, 384 * pp : 384 * (pp + 1)] + bin_ref[...]
            mean = jnp.sum(h * h, axis=-1, keepdims=True) * (1.0 / 384)
            v = silu(h * lax.rsqrt(mean + 1e-6) * gin_ref[...])
            halves.append(v.reshape(4, SC * 4, 8, 384))
        feats = jnp.stack(halves, axis=2)
        t_in = lax.broadcasted_iota(jnp.int32, (4, 1, 1, 1, 1), 0)
        feats = jnp.where(t_in + 2 * frame >= 2, feats, 0.0)
        feats = feats.reshape(4, SC * 64, 384).astype(BF16)
        hist = jnp.concatenate([feats[k : k + 2] for k in range(3)], axis=-1)
        acc = jnp.dot(hist.reshape(2 * SC * 64, 1152), wtime_ref[...], preferred_element_type=F32)
        acc = acc + btime_ref[...]
        acc = acc.reshape(2, SC * 8, 8, 768)
        for v in range(3):
            both = []
            for j in range(2):
                a0 = pltpu.roll(acc[0, :, :, 384 * j : 384 * (j + 1)], 7 - v, 1)
                a1 = pltpu.roll(acc[1, :, :, 384 * j : 384 * (j + 1)], 3 - v, 1)
                both.append(jnp.where(sub[0] < 4, a0, a1))
            full = jnp.concatenate(both, axis=1)
            group = lax.broadcasted_iota(jnp.int32, (1, 16, 1), 1) % 4
            if v == 0:
                full = jnp.where(jnp.logical_and(top, group == 0), 0.0, full)
            if v == 2:
                full = jnp.where(jnp.logical_and(bottom, group == 3), 0.0, full)
            dbl_ref[v, pl.ds(8 * s0 + 1, SC * 8)] = full.astype(BF16)
        return carry

    lax.fori_loop(0, 16 // SC, chunk, 0)


def back(step, place_ref, dbl_ref, wl_ref, bl_ref, gl_ref, wf_ref, bf_ref, out_ref, rows_ref):
    top, bottom = place_ref[0] == 0, place_ref[0] == place_ref[2] - 1
    width = dbl_ref.shape[1] - 2
    x0 = step * XB
    count = XB + 1
    lane = lax.broadcasted_iota(jnp.int32, (1, 1, 128), 2)
    low = lane < 64
    d_m, d_0, d_p = (dbl_ref[v, pl.ds(x0, XB + 2)] for v in range(3))
    group = lax.broadcasted_iota(jnp.int32, (1, 16, 1), 1) % 4
    col = lax.broadcasted_iota(jnp.int32, (count, 1, 1), 0) + (x0 - 1)

    def lift(upper, lower, drop):
        patch = jnp.concatenate([upper[:-1], upper[1:], lower[:-1], lower[1:]], axis=-1)
        acc = jnp.dot(patch.reshape(count * 16, -1), wl_ref[...], preferred_element_type=F32)
        acc = acc.reshape(count, 16, 768) + bl_ref[...]
        out = []
        for px in range(2):
            tiles = [acc[..., 384 * px + 128 * k : 384 * px + 128 * (k + 1)] for k in range(3)]
            sq = [v * v for v in tiles]
            s0 = jnp.sum(sq[0] + jnp.where(low, sq[1], 0.0), axis=-1, keepdims=True)
            s1 = jnp.sum(sq[2] + jnp.where(low, 0.0, sq[1]), axis=-1, keepdims=True)
            f0 = lax.rsqrt(s0 * (1.0 / 192) + 1e-6)
            f1 = lax.rsqrt(s1 * (1.0 / 192) + 1e-6)
            inside = (col >= 0) if px == 0 else (col < width - 1)
            for k, f in enumerate((f0, jnp.where(low, f0, f1), f1)):
                v = silu(tiles[k] * f * gl_ref[:, 384 * px + 128 * k : 384 * px + 128 * (k + 1)])
                keep = inside if drop[k] is None else jnp.logical_and(inside, jnp.logical_not(drop[k]))
                out.append(jnp.where(keep, v, 0.0).astype(BF16))
        return out

    above = jnp.logical_and(group == 0, top)
    below = jnp.logical_and(group == 3, bottom)
    s_m = lift(d_m, d_0, (above, jnp.logical_and(above, low), None))
    s_p = lift(d_0, d_p, (None, jnp.logical_and(below, jnp.logical_not(low)), below))
    s_e = []
    for px in range(2):
        s_e += [s_p[3 * px], jnp.where(low, s_p[3 * px + 1], s_m[3 * px + 1]), s_m[3 * px + 2]]

    def odd(tiles):
        return jnp.concatenate(tiles, axis=-1).reshape(count * 16, 768)

    def even(tiles):
        return jnp.concatenate([v[1:] for v in tiles[:3]] + [v[:-1] for v in tiles[3:]], axis=-1).reshape(XB * 16, 768)

    def mul(lhs, kind, lo, hi):
        return jnp.dot(lhs, wf_ref[kind, :, lo:hi], preferred_element_type=F32).reshape(-1, 16, hi - lo)

    e_o, e_e = mul(odd(s_e), 1, 0, 512), mul(even(s_e), 0, 0, 512)
    results = (
        (mul(odd(s_m), 3, 256, 512), mul(even(s_m), 2, 256, 512)),
        (e_o[..., :256], e_e[..., :256]),
        (e_o[..., 256:], e_e[..., 256:]),
        (mul(odd(s_p), 3, 0, 256), mul(even(s_p), 2, 0, 256)),
    )
    for a, (o, e) in enumerate(results):
        t0 = jnp.where(lane < 96, o[:-1, :, 128:], e[..., :128])
        t1 = e[..., 128:]
        t2 = jnp.where(lane < 32, e[..., :128], o[1:, :, :128])
        for k, t in enumerate((t0, t1, t2)):
            t = t + bf_ref[:, 128 * k : 128 * (k + 1)]
            for u in range(XB):
                rows_ref[3 * u + k, pl.ds(a, 16, stride=4), :] = t[u]
    for j in range(2):
        for t in range(2):
            base = 16 * (2 * j + t)
            for n in range(3 * XB):
                out_ref[2 * t + j, :, 128 * n : 128 * (n + 1)] = rows_ref[n, base : base + 16, :].astype(BF16)


def decode_kernel(
    place_ref, blocks_ref, band_ref, bin_ref, gin_ref, wtime_ref, btime_ref, wl_ref, bl_ref, gl_ref, wf_ref, bf_ref,
    out_ref, grid_ref, dbl_ref, rows_ref,
):
    step = pl.program_id(0)

    @pl.when(step == 0)
    def _():
        front(place_ref, blocks_ref, band_ref, bin_ref, gin_ref, wtime_ref, btime_ref, grid_ref, dbl_ref)

    back(step, place_ref, dbl_ref, wl_ref, bl_ref, gl_ref, wf_ref, bf_ref, out_ref, rows_ref)


def lanes_of_phases(v):
    half = jnp.concatenate([v[:128], v[128:], v[128:], v[:128]])
    return jnp.concatenate([half, half])[None]


def decode(place, blocks, band, wl, wf, b_in, gain_in, w_time, b_time, b_lift, gain_lift, b_final):
    width = 128
    args = (
        blocks, band, b_in[None], gain_in[None], w_time.reshape(1152, 768), b_time[None],
        wl, lanes_of_phases(b_lift), lanes_of_phases(gain_lift), wf, jnp.tile(b_final, 4)[None],
    )

    def whole(a):
        return pl.BlockSpec(a.shape, lambda i: (0,) * a.ndim, pipeline_mode=pl.Buffered(1))

    return pl.pallas_call(
        decode_kernel,
        grid=(width // XB,),
        in_specs=[pl.BlockSpec(memory_space=pltpu.SMEM)] + [whole(a) for a in args],
        out_specs=pl.BlockSpec((4, 16, XB * 384), lambda i: (0, 0, i)),
        out_shape=jax.ShapeDtypeStruct((4, 16, width * 384), BF16),
        scratch_shapes=[
            pltpu.VMEM((6, 18, 8, 128), F32),
            pltpu.VMEM((3, width + 2, 16, 384), BF16),
            pltpu.VMEM((XB * 3, 64, 128), F32),
        ],
        compiler_params=pltpu.CompilerParams(vmem_limit_bytes=56 * 1024 * 1024),
        name="decode",
    )(place, *args)


def turned(block, axis, distance):
    count = lax.axis_size(axis)
    return lax.ppermute(block, axis, [(i, (i + distance) % count) for i in range(count)])


def exchange(latents, tile_slot):
    devices = lax.axis_size("rows") * lax.axis_size("frames")
    slots, width = latents.shape
    owner, inside = tile_slot // slots, tile_slot % slots
    same = owner[:, None] == owner[None, :]
    earlier = jnp.arange(slots)[None, :] < jnp.arange(slots)[:, None]
    rank = jnp.sum(jnp.where(same & earlier, 1, 0), axis=1)
    target = 2 * owner + rank
    pack = (jnp.arange(2 * devices)[:, None] == target[None, :]).astype(BF16)
    tagged = jnp.concatenate([latents, jnp.broadcast_to((inside + 1).astype(BF16)[:, None], (slots, width))], axis=1)
    outgoing = jnp.dot(pack, tagged).reshape(devices, 4 * width)
    arrived = lax.all_to_all(outgoing, ("rows", "frames"), split_axis=0, concat_axis=0, tiled=True)
    arrived = arrived.reshape(2 * devices, 2 * width)
    place = (jnp.arange(1, slots + 1, dtype=jnp.int32)[:, None] == arrived[:, width].astype(jnp.int32)[None, :]).astype(BF16)
    own = jnp.dot(place, arrived[:, :width])
    frames = jnp.stack([turned(own, "frames", 2), turned(own, "frames", 1), own])
    return jnp.stack([turned(frames, "rows", 1), frames, turned(frames, "rows", -1)], axis=1)


def shards(
    latents, tile_slot, w_in, b_in, gain_in, w_time, b_time, w_lift, b_lift, gain_lift, w_final, b_final
):
    place = jnp.stack([lax.axis_index("rows"), lax.axis_index("frames"), lax.axis_size("rows")]).astype(jnp.int32)
    band, wl, wf = make_weights(w_in, w_lift, w_final)
    blocks = exchange(latents, tile_slot)
    return decode(place, blocks, band, wl, wf, b_in, gain_in, w_time, b_time, b_lift, gain_lift, b_final)


def solution(mesh):
    in_specs = (P(("rows", "frames"), None), P(("rows", "frames"))) + (P(),) * 10
    out_specs = P("frames", "rows", None)
    return jax.shard_map(shards, mesh=mesh, in_specs=in_specs, out_specs=out_specs, check_vma=False)
```

profile of v0, /device:TPU:1, one launch (start us, length us, event | category | flops | bytes accessed | tf_op | source)
XLA Modules:
  0.0 89.2 jit_solution(12982913802444120897)
XLA Ops:
  0.1 0.7 and_select_fusion.1
  1.1 0.9 %fusion = bf16[256,256]{1,0:T(8,128)(2,1)S(1)} fusion(bf16[128,128]{1,0:T(8,128)(2,1)S(1)} %broadcast_in_dim.39, bf16[128,128]{1,0:T(8,128)(2,1)} %param.12, s32[128]{0:T(128)S(1)} %multiply_add_fusion), kind=kOutput, calls=%fused_computation.3 | convolution fusion | flops 16941056 | bytes 197120 | tf_op jit(solution)/shard_map/dot_general | solution.py:329
  2.6 1.4 %reduce.3 = bf16[128,512]{1,0:T(8,128)(2,1)S(1)} reduce(bf16[128,1,512]{2,1,0:T(2,128)(2,1)S(1)} %all_to_all.8, bf16[]{:T(256)} %broadcast.46), dimensions={1}, to_apply=%all_to_all.8.reduce_sub_computation | reduce | bytes 262146 | tf_op jit(solution)/shard_map/all_to_all | solution.py:330
  4.0 0.7 reshape.32
  4.7 11.5 %all-to-all-start = ((bf16[128,2,256]{2,1,0:T(2,128)(2,1)}), bf16[128,2,256]{2,1,0:T(2,128)(2,1)S(1)}, u32[]{:S(2)}, u32[]{:S(2)}) async-start(bf16[128,2,256]{2,1,0:T(2,128)(2,1)} %reshape.32), calls=%async_computation | async-start | bytes 262144 | tf_op jit(solution)/shard_map/all_to_all | solution.py:330
  16.2 10.1 %all-to-all-done = bf16[128,2,256]{2,1,0:T(2,128)(2,1)S(1)} async-done(((bf16[128,2,256]{2,1,0:T(2,128)(2,1)}), bf16[128,2,256]{2,1,0:T(2,128)(2,1)S(1)}, u32[]{:S(2)}, u32[]{:S(2)}) %all-to-all-start) | async-done | bytes 131104 | tf_op jit(solution)/shard_map/all_to_all | solution.py:330
  26.4 0.8 reduce
  27.6 0.6 collective-permute-start.1
  28.7 0.6 broadcast_in_dim.40.bin_ref
  29.3 0.6 broadcast_in_dim.41.gin_ref
  29.9 0.7 broadcast_in_dim_tile.3.bf_ref
  30.7 0.6 broadcast_in_dim.44.gl_ref
  31.3 0.6 broadcast_in_dim.43.bl_ref
  31.9 0.6 broadcast_in_dim.42.btime_ref
  32.5 2.5 %copy.29.wlift_ref = bf16[3,3,384,192]{3,2,1,0:T(8,128)(2,1)S(1)} copy(bf16[3,3,384,192]{2,3,1,0:T(8,128)(2,1)} %param.19) | data formatting | bytes 2654208 | tf_op args[7]
  35.1 3.0 %weights.1 = (bf16[768,768]{1,0:T(8,128)(2,1)S(1)}, bf16[1536,768]{1,0:T(8,128)(2,1)S(1)}, bf16[4,768,512]{2,1,0:T(8,128)(2,1)}) custom-call(bf16[3,3,3,16,384]{4,3,2,1,0:T(8,128)(2,1)S(1)} %copy-done.3, bf16[3,3,384,192]{3,2,1,0:T(8,128)(2,1)S(1)} %copy.29.wlift_ref, bf16[3,3,192,96]{3,2,1,0:T(8,128)(2,1)S(1)} %copy-done.2), custom_call_target="tpu_custom_call" | custom-call | tf_op jit(solution)/shard_map/weights/pallas_call | solution.py:105
  38.1 1.5 %copy-done = bf16[1536,768]{1,0:T(8,128)(2,1)} copy-done((bf16[1536,768]{1,0:T(8,128)(2,1)}, bf16[1536,768]{1,0:T(8,128)(2,1)S(1)}, u32[]{:S(2)}) %copy-start) | copy-done | bytes 2359320
  39.5 1.0 %copy-done.1 = bf16[768,768]{1,0:T(8,128)(2,1)} copy-done((bf16[768,768]{1,0:T(8,128)(2,1)}, bf16[768,768]{1,0:T(8,128)(2,1)S(1)}, u32[]{:S(2)}) %copy-start.1) | copy-done | bytes 1179672
  40.6 1.2 %collective-permute-start.3 = (bf16[3,128,128]{2,1,0:T(8,128)(2,1)S(1)}, bf16[3,128,128]{2,1,0:T(8,128)(2,1)S(1)}, u32[]{:S(2)}, u32[]{:S(2)}) collective-permute-start(bf16[3,128,128]{2,1,0:T(8,128)(2,1)S(1)} %get-tuple-element.12), channel_id=1, source_target_pairs={{0,112},{16,0},{32,16},{48,32},{64,48},{80,64},{96,80},{112,96},{1... | collective-permute-start | bytes 294920 | tf_op jit(solution)/shard_map/ppermute | solution.py:316
  42.2 0.6 pad_add_fusion.place_ref
  42.8 2.2 %collective-permute-done.3 = bf16[3,128,128]{2,1,0:T(8,128)(2,1)S(1)} collective-permute-done((bf16[3,128,128]{2,1,0:T(8,128)(2,1)S(1)}, bf16[3,128,128]{2,1,0:T(8,128)(2,1)S(1)}, u32[]{:S(2)}, u32[]{:S(2)}) %collective-permute-start.3) | collective-permute-done | bytes 98336 | tf_op jit(solution)/shard_map/ppermute | solution.py:316
  45.0 2.9 %collective-permute-done.2 = bf16[3,128,128]{2,1,0:T(8,128)(2,1)S(1)} collective-permute-done((bf16[3,128,128]{2,1,0:T(8,128)(2,1)S(1)}, bf16[3,128,128]{2,1,0:T(8,128)(2,1)S(1)}, u32[]{:S(2)}, u32[]{:S(2)}) %collective-permute-start.2) | collective-permute-done | bytes 98336 | tf_op jit(solution)/shard_map/ppermute | solution.py:316
  47.9 0.7 pad_maximum_fusion.blocks_ref
  48.7 40.5 %decode.1 = bf16[4,16,49152]{2,1,0:T(8,128)(2,1)} custom-call(s32[3]{0:T(128)} %pad_add_fusion.place_ref, bf16[3,3,128,128]{3,2,1,0:T(8,128)(2,1)} %pad_maximum_fusion.blocks_ref, bf16[768,768]{1,0:T(8,128)(2,1)} %copy-done.1, f32[1,384]{1,0:T(1,128)} %broadcast_in_dim.40.bin_ref, f32[1,384]{1,0:T(1,128)} %broadcast_in_dim.41.gin_ref, ...), custom_call_target="tpu_custom_call" | custom-call | tf_op jit(solution)/shard_map/decode/pallas_call | solution.py:298
  (42 shorter events, 2.3 us)
Async XLA Ops:
  0.0 28.7 %copy-start.6 = (f32[192]{0:T(256)S(1)}, f32[192]{0:T(256)}, u32[]{:S(2)}) copy-start(f32[192]{0:T(256)} %param.20) | copy-start | bytes 2308
  0.0 31.2 %slice-start.1 = ((f32[192]{0:T(256)}), f32[128]{0:T(128)S(1)}, s32[]{:S(2)}) async-start(f32[192]{0:T(256)} %param.20), calls=%async_computation.2 | async-start | bytes 1024 | tf_op jit(solution)/shard_map/slice | solution.py:284
  0.0 28.7 %copy-start.5 = (f32[192]{0:T(256)S(1)}, f32[192]{0:T(256)}, u32[]{:S(2)}) copy-start(f32[192]{0:T(256)} %param.21) | copy-start | bytes 2308
  0.0 30.6 %slice-start = ((f32[192]{0:T(256)}), f32[128]{0:T(128)S(1)}, s32[]{:S(2)}) async-start(f32[192]{0:T(256)} %param.21), calls=%async_computation.1 | async-start | bytes 1024 | tf_op jit(solution)/shard_map/slice | solution.py:284
  0.0 28.7 %copy-start.7 = (f32[384]{0:T(512)S(1)}, f32[384]{0:T(512)}, u32[]{:S(2)}) copy-start(f32[384]{0:T(512)} %param.15) | copy-start | bytes 4612
  0.0 29.3 %copy-start.8 = (f32[384]{0:T(512)S(1)}, f32[384]{0:T(512)}, u32[]{:S(2)}) copy-start(f32[384]{0:T(512)} %param.16) | copy-start | bytes 4612
  0.0 29.9 %copy-start.9 = (f32[96]{0:T(128)S(1)}, f32[96]{0:T(128)}, u32[]{:S(2)}) copy-start(f32[96]{0:T(128)} %param.23) | copy-start | bytes 1156
  0.1 31.9 %copy-start.4 = (f32[768]{0:T(1024)S(1)}, f32[768]{0:T(1024)}, u32[]{:S(2)}) copy-start(f32[768]{0:T(1024)} %param.18) | copy-start | bytes 9220
  4.7 21.7 %all-to-all-start = ((bf16[128,2,256]{2,1,0:T(2,128)(2,1)}), bf16[128,2,256]{2,1,0:T(2,128)(2,1)S(1)}, u32[]{:S(2)}, u32[]{:S(2)}) async-start(bf16[128,2,256]{2,1,0:T(2,128)(2,1)} %reshape.32), calls=%async_computation | async-start | bytes 262144 | tf_op jit(solution)/shard_map/all_to_all | solution.py:330
  27.2 7.8 %copy-start.2 = (bf16[3,3,192,96]{3,2,1,0:T(8,128)(2,1)S(1)}, bf16[3,3,192,96]{3,2,1,0:T(8,128)(2,1)}, u32[]{:S(2)}) copy-start(bf16[3,3,192,96]{3,2,1,0:T(8,128)(2,1)} %wfinal_ref.1) | copy-start | bytes 995332
  27.2 7.8 %copy-start.3 = (bf16[3,3,3,16,384]{4,3,2,1,0:T(8,128)(2,1)S(1)}, bf16[3,3,3,16,384]{4,3,2,1,0:T(8,128)(2,1)}, u32[]{:S(2)}) copy-start(bf16[3,3,3,16,384]{4,3,2,1,0:T(8,128)(2,1)} %win_ref.1) | copy-start | bytes 995332
  27.6 12.9 %collective-permute-start.1 = (bf16[128,128]{1,0:T(8,128)(2,1)S(1)}, bf16[128,128]{1,0:T(8,128)(2,1)S(1)}, u32[]{:S(2)}, u32[]{:S(2)}) collective-permute-start(bf16[128,128]{1,0:T(8,128)(2,1)S(1)} %fusion.1), channel_id=1, source_target_pairs={{0,1},{1,2},{2,3},{3,4},{4,5},{5,6},{6,7},{7,8},{8,9},{9,10},{10,1... | collective-permute-start | bytes 98312 | tf_op jit(solution)/shard_map/ppermute | solution.py:316
  28.3 12.3 %collective-permute-start = (bf16[128,128]{1,0:T(8,128)(2,1)S(1)}, bf16[128,128]{1,0:T(8,128)(2,1)S(1)}, u32[]{:S(2)}, u32[]{:S(2)}) collective-permute-start(bf16[128,128]{1,0:T(8,128)(2,1)S(1)} %fusion.1), channel_id=1, source_target_pairs={{0,2},{1,3},{2,4},{3,5},{4,6},{5,7},{6,8},{7,9},{8,10},{9,11},{10,... | collective-permute-start | bytes 98312 | tf_op jit(solution)/shard_map/ppermute | solution.py:316
  38.1 1.5 %copy-start = (bf16[1536,768]{1,0:T(8,128)(2,1)}, bf16[1536,768]{1,0:T(8,128)(2,1)S(1)}, u32[]{:S(2)}) copy-start(bf16[1536,768]{1,0:T(8,128)(2,1)S(1)} %get-tuple-element.9.wl_ref) | copy-start | bytes 7077892
  39.5 1.0 %copy-start.1 = (bf16[768,768]{1,0:T(8,128)(2,1)}, bf16[768,768]{1,0:T(8,128)(2,1)S(1)}, u32[]{:S(2)}) copy-start(bf16[768,768]{1,0:T(8,128)(2,1)S(1)} %get-tuple-element.8.band_ref) | copy-start | bytes 3538948
  40.6 4.4 %collective-permute-start.3 = (bf16[3,128,128]{2,1,0:T(8,128)(2,1)S(1)}, bf16[3,128,128]{2,1,0:T(8,128)(2,1)S(1)}, u32[]{:S(2)}, u32[]{:S(2)}) collective-permute-start(bf16[3,128,128]{2,1,0:T(8,128)(2,1)S(1)} %get-tuple-element.12), channel_id=1, source_target_pairs={{0,112},{16,0},{32,16},{48,32},{64,48},{80,64},{96,80},{112,96},{1... | collective-permute-start | bytes 294920 | tf_op jit(solution)/shard_map/ppermute | solution.py:316
  41.8 6.1 %collective-permute-start.2 = (bf16[3,128,128]{2,1,0:T(8,128)(2,1)S(1)}, bf16[3,128,128]{2,1,0:T(8,128)(2,1)S(1)}, u32[]{:S(2)}, u32[]{:S(2)}) collective-permute-start(bf16[3,128,128]{2,1,0:T(8,128)(2,1)S(1)} %get-tuple-element.12), channel_id=1, source_target_pairs={{0,16},{16,32},{32,48},{48,64},{64,80},{80,96},{96,112},{112,0},{1... | collective-permute-start | bytes 294920 | tf_op jit(solution)/shard_map/ppermute | solution.py:316
where the time goes:
time: 89.5 us; the launch traced here: 89.2 us
  Pallas kernels  43.5 us (49%)
  waiting for transfers between devices  15.3 us (17%)
  starting transfers between devices  14.1 us (16%)
  local copies, waits for them, and re-layouts  10.3 us (12%)
  other arithmetic  4.6 us (5%)
  matrix products  1.14 us (1%)
    pallas_call x1, Pallas kernels, decode(): pl.pallas_call(decode_kernel, grid=(width // XB,), in_specs=[pl.BlockSpec...  40.5 us
    all_to_all x1, starting transfers between devices, exchange(): lax.all_to_all(outgoing, ('rows', 'frames'), split_axis=0, concat_axis=0,...  11.5 us
    all_to_all x1, waiting for transfers between devices, exchange(): lax.all_to_all(outgoing, ('rows', 'frames'), split_axis=0, concat_axis=0,...  10.1 us
    unnamed x23, local copies, waits for them, and re-layouts  5.85 us
    ppermute x4, waiting for transfers between devices, turned(): lax.ppermute(block, axis, [(i, (i + distance) % count) for i in range(cou...  5.11 us
    pallas_call x1, Pallas kernels, make_weights(): pl.pallas_call(weights_kernel, in_specs=[whole] * 3, out_specs=[whole] *...  2.99 us
    ppermute x4, starting transfers between devices, turned(): lax.ppermute(block, axis, [(i, (i + distance) % count) for i in range(cou...  2.61 us
    all_to_all x2, other arithmetic, exchange(): lax.all_to_all(outgoing, ('rows', 'frames'), split_axis=0, concat_axis=0,...  2.16 us
  transfers between devices with their start and end apart: 5, of which 3 were waited for; matrix products, arithmetic and copies ran while one was open for 8% of the time, Pallas kernels for 3%

commit v1 on v0

--- a/solution.py
+++ b/solution.py
@@ -28,7 +28,7 @@
     return pick(rows, tx, px)
 
 
-def weights_kernel(win_ref, wlift_ref, wfinal_ref, band_ref, lift_ref, final_ref):
+def make_band(win_ref, band_ref):
     channels = win_ref.shape[-1]
     band_ref[...] = jnp.zeros_like(band_ref)
     for k in range(3):
@@ -38,93 +38,63 @@
                 for pp in range(2):
                     row = 256 * k + 64 * dy + 16 * (dx + pp)
                     band_ref[row : row + 16, channels * pp : channels * (pp + 1)] = taps
-    depth = wlift_ref.shape[2]
-
-    def lift_rows(step, carry):
-        row = pl.multiple_of(step * 64, 64)
-
-        def wide(dy, dx):
-            return wlift_ref[dy, dx, pl.ds(row, 64), 0:128].astype(F32)
-
-        def narrow(dy, dx):
-            return wlift_ref[dy, dx, pl.ds(row, 64), 128:192].astype(F32)
-
-        for ty in range(2):
-            for tx in range(2):
-                for px in range(2):
-                    tiles = [
-                        summed_taps(wide, ty, tx, 0, px),
-                        jnp.concatenate([summed_taps(narrow, ty, tx, py, px) for py in range(2)], axis=-1),
-                        summed_taps(wide, ty, tx, 1, px),
-                    ]
-                    for n, tile in enumerate(tiles):
-                        lane = 384 * px + 128 * n
-                        lift_ref[pl.ds(depth * (2 * ty + tx) + row, 64), lane : lane + 128] = tile.astype(BF16)
-        return carry
-
-    lax.fori_loop(0, depth // 64, lift_rows, 0)
-
-    def final_rows(part):
-        rows = slice(64 * part, 64 * (part + 1))
-        low = lax.broadcasted_iota(jnp.int32, (64, 128), 1) < 64
-        pad = jnp.zeros((64, 32), F32)
-
-        def load(dy, dx):
-            return wfinal_ref[dy, dx, rows, :].astype(F32)
-
-        for ty in range(2):
-            for tx in range(2):
-                for qy in range(2):
-                    q0, q1 = (
-                        jnp.concatenate([summed_taps(load, ty, tx, qy, qx), pad], axis=-1) for qx in range(2)
-                    )
-                    r0, r1 = pltpu.roll(q0, 96, 1), pltpu.roll(q1, 64, 1)
-                    pairs = (
-                        (jnp.where(low, r1, r0), jnp.where(low, r0, r1)),
-                        (pltpu.roll(q0, 32, 1), q1),
-                    )
-                    for xpar, tiles in enumerate(pairs):
-                        px = tx if xpar else 1 - tx
-                        for jpar in range(2):
-                            py = ty if jpar else 1 - ty
-                            slot = 384 * px
-                            if part < 2:
-                                slot += 256 * py + 64 * part
-                            else:
-                                slot += 128 + 64 * py
-                            for n, tile in enumerate(tiles):
-                                lane = 256 * qy + 128 * n
-                                final_ref[2 * jpar + xpar, slot : slot + 64, lane : lane + 128] = tile.astype(BF16)
-
-    for part in range(3):
-        final_rows(part)
-
-
-def make_weights(w_in, w_lift, w_final):
-    whole = pl.BlockSpec(memory_space=pltpu.VMEM)
-    return pl.pallas_call(
-        weights_kernel,
-        in_specs=[whole] * 3,
-        out_specs=[whole] * 3,
-        out_shape=[
-            jax.ShapeDtypeStruct((768, 768), BF16),
-            jax.ShapeDtypeStruct((1536, 768), BF16),
-            jax.ShapeDtypeStruct((4, 768, 512), BF16),
-        ],
-        compiler_params=pltpu.CompilerParams(vmem_limit_bytes=48 * 1024 * 1024),
-        name="weights",
-    )(w_in, w_lift, w_final)
-
-
-def front(place_ref, blocks_ref, band_ref, bin_ref, gin_ref, wtime_ref, btime_ref, grid_ref, dbl_ref):
-    row, frame = place_ref[0], place_ref[1]
-    top, bottom = row == 0, row == place_ref[2] - 1
-    out_row = lax.broadcasted_iota(jnp.int32, (256, 384), 0)
-    in_row = lax.broadcasted_iota(jnp.int32, (256, 384), 1)
-    y_in = out_row % 8 + 2
-    wanted = (y_in // 4) * 128 + (out_row // 128) * 64 + (y_in % 4) * 16 + (out_row // 8) % 16
+
+
+def make_lift(wlift_ref, lift_ref, ty, tx):
+    depth = wlift_ref.shape[-1]
+
+    def part(lo, hi, py, px):
+        return summed_taps(lambda dy, dx: wlift_ref[dy, dx, lo:hi, :].astype(F32), ty, tx, py, px)
+
+    for px in range(2):
+        tiles = [
+            part(0, 128, 0, px),
+            jnp.concatenate([part(128, 192, 0, px), part(128, 192, 1, px)], axis=0),
+            part(0, 128, 1, px),
+        ]
+        for n, tile in enumerate(tiles):
+            lane = 384 * px + 128 * n
+            row = depth * (2 * ty + tx)
+            lift_ref[row : row + depth, lane : lane + 128] = tile.T.astype(BF16)
+
+
+def make_final(wfinal_ref, final_ref, part):
+    rows = slice(64 * part, 64 * (part + 1))
+    low = lax.broadcasted_iota(jnp.int32, (64, 128), 1) < 64
+    pad = jnp.zeros((64, 32), F32)
+
+    def load(dy, dx):
+        return wfinal_ref[dy, dx, rows, :].astype(F32)
+
+    for ty in range(2):
+        for tx in range(2):
+            for qy in range(2):
+                q0, q1 = (jnp.concatenate([summed_taps(load, ty, tx, qy, qx), pad], axis=-1) for qx in range(2))
+                r0, r1 = pltpu.roll(q0, 96, 1), pltpu.roll(q1, 64, 1)
+                pairs = ((jnp.where(low, r1, r0), jnp.where(low, r0, r1)), (pltpu.roll(q0, 32, 1), q1))
+                for xpar, tiles in enumerate(pairs):
+                    px = tx if xpar else 1 - tx
+                    for jpar in range(2):
+                        py = ty if jpar else 1 - ty
+                        slot = 384 * px + (256 * py + 64 * part if part < 2 else 128 + 64 * py)
+                        for n, tile in enumerate(tiles):
+                            lane = 256 * qy + 128 * n
+                            final_ref[2 * jpar + xpar, slot : slot + 64, lane : lane + 128] = tile.astype(BF16)
+
+
+def front(blocks_ref, band_ref, bin_ref, gin_ref, wtime_ref, btime_ref, grid_ref, dbl_ref):
+    row, frame = lax.axis_index("rows"), lax.axis_index("frames")
+    top, bottom = row == 0, row == lax.axis_size("rows") - 1
+    out_row = lax.broadcasted_iota(jnp.int32, (256, 256), 0)
+    in_row = lax.broadcasted_iota(jnp.int32, (256, 256), 1)
+    t, s, y = out_row // 128, (out_row // 8) % 16, out_row % 8
+    wanted = jnp.where(
+        y < 2,
+        32 * t + 16 * y + s,
+        jnp.where(y < 6, 64 + 64 * t + 16 * (y - 2) + s, 192 + 32 * t + 16 * (y - 6) + s),
+    )
     inside = jnp.logical_and(
-        jnp.logical_or(jnp.logical_not(top), y_in >= 4), jnp.logical_or(jnp.logical_not(bottom), y_in < 8)
+        jnp.logical_or(jnp.logical_not(top), y >= 2), jnp.logical_or(jnp.logical_not(bottom), y < 6)
     )
     chosen = jnp.logical_and(in_row == wanted, inside)
     zero_col = jnp.zeros((6, 1, 8, 128), F32)
@@ -132,8 +102,7 @@
     grid_ref[:, 17:18] = zero_col
     for part in range(3):
         select = jnp.where(jnp.logical_and(chosen, frame + part >= 2), 1.0, 0.0).astype(BF16)
-        cells = blocks_ref[part].reshape(384, 128)
-        picked = jnp.dot(select, cells, preferred_element_type=F32)
+        picked = jnp.dot(select, blocks_ref[part], preferred_element_type=F32)
         grid_ref[2 * part : 2 * part + 2, 1:17] = picked.reshape(2, 16, 8, 128)
 
     lane = lax.broadcasted_iota(jnp.int32, (1, 1, 1, 128), 3)
@@ -198,8 +167,9 @@
     lax.fori_loop(0, 16 // SC, chunk, 0)
 
 
-def back(step, place_ref, dbl_ref, wl_ref, bl_ref, gl_ref, wf_ref, bf_ref, out_ref, rows_ref):
-    top, bottom = place_ref[0] == 0, place_ref[0] == place_ref[2] - 1
+def back(step, dbl_ref, wl_ref, bl_ref, gl_ref, wf_ref, bf_ref, out_ref, rows_ref):
+    row = lax.axis_index("rows")
+    top, bottom = row == 0, row == lax.axis_size("rows") - 1
     width = dbl_ref.shape[1] - 2
     x0 = step * XB
     count = XB + 1
@@ -268,16 +238,16 @@
 
 
 def decode_kernel(
-    place_ref, blocks_ref, band_ref, bin_ref, gin_ref, wtime_ref, btime_ref, wl_ref, bl_ref, gl_ref, wf_ref, bf_ref,
+    blocks_ref, band_ref, bin_ref, gin_ref, wtime_ref, btime_ref, wl_ref, bl_ref, gl_ref, wf_ref, bf_ref,
     out_ref, grid_ref, dbl_ref, rows_ref,
 ):
     step = pl.program_id(0)
 
     @pl.when(step == 0)
     def _():
-        front(place_ref, blocks_ref, band_ref, bin_ref, gin_ref, wtime_ref, btime_ref, grid_ref, dbl_ref)
-
-    back(step, place_ref, dbl_ref, wl_ref, bl_ref, gl_ref, wf_ref, bf_ref, out_ref, rows_ref)
+        front(blocks_ref, band_ref, bin_ref, gin_ref, wtime_ref, btime_ref, grid_ref, dbl_ref)
+
+    back(step, dbl_ref, wl_ref, bl_ref, gl_ref, wf_ref, bf_ref, out_ref, rows_ref)
 
 
 def lanes_of_phases(v):
@@ -285,7 +255,7 @@
     return jnp.concatenate([half, half])[None]
 
 
-def decode(place, blocks, band, wl, wf, b_in, gain_in, w_time, b_time, b_lift, gain_lift, b_final):
+def decode(blocks, band, wl, wf, b_in, gain_in, w_time, b_time, b_lift, gain_lift, b_final):
     width = 128
     args = (
         blocks, band, b_in[None], gain_in[None], w_time.reshape(1152, 768), b_time[None],
@@ -298,7 +268,7 @@
     return pl.pallas_call(
         decode_kernel,
         grid=(width // XB,),
-        in_specs=[pl.BlockSpec(memory_space=pltpu.SMEM)] + [whole(a) for a in args],
+        in_specs=[whole(a) for a in args],
         out_specs=pl.BlockSpec((4, 16, XB * 384), lambda i: (0, 0, i)),
         out_shape=jax.ShapeDtypeStruct((4, 16, width * 384), BF16),
         scratch_shapes=[
@@ -308,40 +278,165 @@
         ],
         compiler_params=pltpu.CompilerParams(vmem_limit_bytes=56 * 1024 * 1024),
         name="decode",
-    )(place, *args)
-
-
-def turned(block, axis, distance):
-    count = lax.axis_size(axis)
-    return lax.ppermute(block, axis, [(i, (i + distance) % count) for i in range(count)])
-
-
-def exchange(latents, tile_slot):
-    devices = lax.axis_size("rows") * lax.axis_size("frames")
-    slots, width = latents.shape
-    owner, inside = tile_slot // slots, tile_slot % slots
-    same = owner[:, None] == owner[None, :]
-    earlier = jnp.arange(slots)[None, :] < jnp.arange(slots)[:, None]
-    rank = jnp.sum(jnp.where(same & earlier, 1, 0), axis=1)
-    target = 2 * owner + rank
-    pack = (jnp.arange(2 * devices)[:, None] == target[None, :]).astype(BF16)
-    tagged = jnp.concatenate([latents, jnp.broadcast_to((inside + 1).astype(BF16)[:, None], (slots, width))], axis=1)
-    outgoing = jnp.dot(pack, tagged).reshape(devices, 4 * width)
-    arrived = lax.all_to_all(outgoing, ("rows", "frames"), split_axis=0, concat_axis=0, tiled=True)
-    arrived = arrived.reshape(2 * devices, 2 * width)
-    place = (jnp.arange(1, slots + 1, dtype=jnp.int32)[:, None] == arrived[:, width].astype(jnp.int32)[None, :]).astype(BF16)
-    own = jnp.dot(place, arrived[:, :width])
-    frames = jnp.stack([turned(own, "frames", 2), turned(own, "frames", 1), own])
-    return jnp.stack([turned(frames, "rows", 1), frames, turned(frames, "rows", -1)], axis=1)
+    )(*args)
+
+
+def exchange_kernel(
+    rows, frames,
+    lat_ref, slot_ref, win_hbm, wlift_hbm, wfinal_hbm,
+    blocks_ref, band_hbm, lift_hbm, final_hbm,
+    send1, recv1, send2, recv2, above, own, below, win_ref, wlift_ref, wfinal_ref, band_ref, lift_ref, final_ref,
+    load_sem, store_sem, send_sem1, recv_sem1, send_sem2, recv_sem2, send_sem3, recv_sem3,
+):
+    r, f = lax.axis_index("rows"), lax.axis_index("frames")
+    loads = [
+        pltpu.make_async_copy(src, dst, load_sem.at[n])
+        for n, (src, dst) in enumerate(((win_hbm, win_ref), (wlift_hbm, wlift_ref), (wfinal_hbm, wfinal_ref)))
+    ]
+    for copy in loads:
+        copy.start()
+
+    def at(dr, df):
+        return {"rows": lax.rem(r + dr + rows, rows), "frames": lax.rem(f + df + frames, frames)}
+
+    near = [(dr, df) for df in range(3) for dr in (0, 1, -1) if (dr, df) != (0, 0)]
+    far = [(dr, df) for dr, df in near if dr != 0 and df != 0]
+    barrier = pltpu.get_barrier_semaphore()
+    sources = [(k, 0) for k in range(1, rows)] + [(0, k) for k in range(1, frames)] + [(-dr, -df) for dr, df in far]
+    for dr, df in sources:
+        pl.semaphore_signal(barrier, inc=1, device_id=at(dr, df), device_id_type=pl.DeviceIdType.MESH)
+
+    slots, width = lat_ref.shape
+    across = jnp.broadcast_to(slot_ref[...].reshape(1, slots), (slots, slots))
+    down = across.T
+    index = lax.broadcasted_iota(jnp.int32, (slots, slots), 0)
+    lane = lax.broadcasted_iota(jnp.int32, (slots, slots), 1)
+    twin = jnp.logical_and(across // slots == down // slots, index < lane)
+    rank = jnp.sum(jnp.where(twin, 1, 0), axis=0, keepdims=True)
+    target = 2 * (across[:1] // slots) + rank
+    total = 2 * rows * frames
+    place = lax.broadcasted_iota(jnp.int32, (total, slots), 0) == target
+    tags = (down % slots + 1).astype(F32).astype(BF16)
+    tagged = jnp.concatenate([lat_ref[...], tags], axis=-1)
+    packed = jnp.dot(jnp.where(place, 1.0, 0.0).astype(BF16), tagged, preferred_element_type=F32)
+    send1[...] = packed.astype(BF16).reshape(send1.shape)
+    recv1[r] = send1[r]
+    pl.semaphore_wait(barrier, len(sources))
+
+    def remote(src, dst, send, recv, dr, df):
+        return pltpu.make_async_remote_copy(
+            src_ref=src, dst_ref=dst, send_sem=send, recv_sem=recv,
+            device_id=at(dr, df), device_id_type=pl.DeviceIdType.MESH,
+        )
+
+    first = []
+    for k in range(1, rows):
+        peer, source = lax.rem(r + k, rows), lax.rem(r - k + rows, rows)
+        out = remote(send1.at[peer], recv1.at[r], send_sem1.at[k], recv_sem1.at[k], k, 0)
+        out.start()
+        first.append((out, remote(send1.at[peer], recv1.at[source], send_sem1.at[k], recv_sem1.at[k], k, 0)))
+    loads[0].wait()
+    make_band(win_ref, band_ref)
+    loads[1].wait()
+    make_lift(wlift_ref, lift_ref, 0, 0)
+    for out, arrival in first:
+        arrival.wait_recv()
+
+    o = lax.broadcasted_iota(jnp.int32, (total, total), 0)
+    i = lax.broadcasted_iota(jnp.int32, (total, total), 1)
+    group = 2 * rows
+    regroup = i == ((o // 2) % rows) * (2 * frames) + (o // group) * 2 + o % 2
+    moved = jnp.dot(
+        jnp.where(regroup, 1.0, 0.0).astype(BF16), recv1[...].reshape(total, 2 * width), preferred_element_type=F32
+    )
+    send2[...] = moved.astype(BF16).reshape(send2.shape)
+    recv2[f] = send2[f]
+    second = []
+    for k in range(1, frames):
+        peer, source = lax.rem(f + k, frames), lax.rem(f - k + frames, frames)
+        out = remote(send2.at[peer], recv2.at[f], send_sem2.at[k], recv_sem2.at[k], 0, k)
+        out.start()
+        second.append((out, remote(send2.at[peer], recv2.at[source], send_sem2.at[k], recv_sem2.at[k], 0, k)))
+    make_lift(wlift_ref, lift_ref, 0, 1)
+    make_lift(wlift_ref, lift_ref, 1, 0)
+    for out, arrival in second:
+        arrival.wait_recv()
+
+    arrived = recv2[...].reshape(total, 2 * width)
+    want = lax.broadcasted_iota(jnp.int32, (total, slots), 1).astype(F32) + 1.0
+    land = jnp.where(arrived[:, width:].astype(F32) == want, 1.0, 0.0).astype(BF16)
+    canvas = lax.dot_general(land, arrived[:, :width], (((0,), (0,)), ((), ())), preferred_element_type=F32)
+    own[2] = canvas.astype(BF16).reshape(2, 64, width)
+    third = []
+    for n, (dr, df) in enumerate(near):
+        src, region = {
+            0: (own.at[2], own),
+            1: (own.at[2, :, pl.ds(32, 32)], above),
+            -1: (own.at[2, :, pl.ds(0, 32)], below),
+        }[dr]
+        out = remote(src, region.at[2 - df], send_sem3.at[n], recv_sem3.at[n], dr, df)
+        out.start()
+        third.append(out)
+    make_lift(wlift_ref, lift_ref, 1, 1)
+    loads[2].wait()
+    for part in range(3):
+        make_final(wfinal_ref, final_ref, part)
+    stores = [
+        pltpu.make_async_copy(src, dst, store_sem.at[n])
+        for n, (src, dst) in enumerate(((band_ref, band_hbm), (lift_ref, lift_hbm), (final_ref, final_hbm)))
+    ]
+    for copy in stores:
+        copy.start()
+    for out in third:
+        out.wait_recv()
+    for part in range(3):
+        blocks_ref[part, 0:64] = above[part].reshape(64, width)
+        blocks_ref[part, 64:192] = own[part].reshape(128, width)
+        blocks_ref[part, 192:256] = below[part].reshape(64, width)
+    for out, _ in first + second:
+        out.wait_send()
+    for out in third:
+        out.wait_send()
+    for copy in stores:
+        copy.wait()
+
+
+def exchange(latents, tile_slot, w_in, w_lift, w_final):
+    rows, frames = lax.axis_size("rows"), lax.axis_size("frames")
+    width = latents.shape[1]
+    vmem, hbm = pl.BlockSpec(memory_space=pltpu.VMEM), pl.BlockSpec(memory_space=pltpu.HBM)
+    weights = (w_in, w_lift.swapaxes(2, 3), w_final)
+    made = [(768, 768), (1536, 768), (4, 768, 512)]
+    dma = pltpu.SemaphoreType.DMA
+    return pl.pallas_call(
+        functools.partial(exchange_kernel, rows, frames),
+        in_specs=[vmem, vmem, hbm, hbm, hbm],
+        out_specs=[vmem, hbm, hbm, hbm],
+        out_shape=[jax.ShapeDtypeStruct(shape, BF16) for shape in [(3, 256, width)] + made],
+        scratch_shapes=[
+            pltpu.VMEM((rows, 2 * frames, 2 * width), BF16),
+            pltpu.VMEM((rows, 2 * frames, 2 * width), BF16),
+            pltpu.VMEM((frames, 2 * rows, 2 * width), BF16),
+            pltpu.VMEM((frames, 2 * rows, 2 * width), BF16),
+            pltpu.VMEM((3, 2, 32, width), BF16),
+            pltpu.VMEM((3, 2, 64, width), BF16),
+            pltpu.VMEM((3, 2, 32, width), BF16),
+        ]
+        + [pltpu.VMEM(w.shape, BF16) for w in weights]
+        + [pltpu.VMEM(shape, BF16) for shape in made]
+        + [dma((3,)), dma((3,)), dma((rows,)), dma((rows,)), dma((frames,)), dma((frames,)), dma((8,)), dma((8,))],
+        compiler_params=pltpu.CompilerParams(
+            collective_id=0, has_side_effects=True, vmem_limit_bytes=40 * 1024 * 1024
+        ),
+        name="exchange",
+    )(latents, tile_slot, *weights)
 
 
 def shards(
     latents, tile_slot, w_in, b_in, gain_in, w_time, b_time, w_lift, b_lift, gain_lift, w_final, b_final
 ):
-    place = jnp.stack([lax.axis_index("rows"), lax.axis_index("frames"), lax.axis_size("rows")]).astype(jnp.int32)
-    band, wl, wf = make_weights(w_in, w_lift, w_final)
-    blocks = exchange(latents, tile_slot)
-    return decode(place, blocks, band, wl, wf, b_in, gain_in, w_time, b_time, b_lift, gain_lift, b_final)
+    blocks, band, wl, wf = exchange(latents, tile_slot, w_in, w_lift, w_final)
+    return decode(blocks, band, wl, wf, b_in, gain_in, w_time, b_time, b_lift, gain_lift, b_final)
 
 
 def solution(mesh):

time: 89.5 us -> 87.2 us (0.974)
  Pallas kernels: 43.5 us -> 66.4 us
  waiting for transfers between devices: 15.3 us -> 0 us
  starting transfers between devices: 14.1 us -> 0 us
  local copies, waits for them, and re-layouts: 10.3 us -> 20.3 us
  other arithmetic: 4.6 us -> 0 us
  matrix products: 1.14 us -> 0 us
    pallas_call x2, Pallas kernels: 43.5 us -> 66.4 us  [the longest x1 40.3 us: decode(): pl.pallas_call(decode_kernel, grid=(width // XB,), in_specs=[whole(a) for...]
    all_to_all x1 -> x0, starting transfers between devices: 11.5 us -> none  [exchange(): lax.all_to_all(outgoing, ('rows', 'frames'), split_axis=0, concat_axis=0,...]
    all_to_all x1 -> x0, waiting for transfers between devices: 10.1 us -> none  [exchange(): lax.all_to_all(outgoing, ('rows', 'frames'), split_axis=0, concat_axis=0,...]
    ppermute x4 -> x0, waiting for transfers between devices: 5.11 us -> none  [turned(): lax.ppermute(block, axis, [(i, (i + distance) % count) for i in range(cou...]
    unnamed x23 -> x18, local copies, waits for them, and re-layouts: 5.85 us -> 9.57 us
    slice x6 -> x4, local copies, waits for them, and re-layouts: 0.02 us -> 2.72 us  [lanes_of_phases(): half = jnp.concatenate([v[:128], v[128:], v[128:], v[:128]])]
    ppermute x4 -> x0, starting transfers between devices: 2.61 us -> none  [turned(): lax.ppermute(block, axis, [(i, (i + distance) % count) for i in range(cou...]
    all_to_all x2 -> x0, other arithmetic: 2.16 us -> none  [exchange(): lax.all_to_all(outgoing, ('rows', 'frames'), split_axis=0, concat_axis=0,...]
  transfers between devices with their start and end apart: 5 -> 0, of which waited for: 3 -> 0; matrix products, arithmetic and copies ran while one was open for 8% -> 0% of each run, Pallas kernels for 3% -> 0%
where the time goes in v1:
time: 87.2 us; the launch traced here: 86.7 us
  Pallas kernels  66.4 us (76%)
  local copies, waits for them, and re-layouts  20.3 us (23%)
    pallas_call x1, Pallas kernels, decode(): pl.pallas_call(decode_kernel, grid=(width // XB,), in_specs=[whole(a) for...  40.3 us
    pallas_call x1, Pallas kernels, exchange(): pl.pallas_call(functools.partial(exchange_kernel, rows, frames), in_specs...  26 us
    unnamed x18, local copies, waits for them, and re-layouts  9.57 us
    slice x4, local copies, waits for them, and re-layouts, lanes_of_phases(): half = jnp.concatenate([v[:128], v[128:], v[128:], v[:128]])  2.72 us

profile of v1, /device:TPU:1, one launch (start us, length us, event | category | flops | bytes accessed | tf_op | source)
XLA Modules:
  0.0 86.7 jit_solution(6950092078688527582)
XLA Ops:
  0.0 0.7 slice.20
  0.7 0.7 slice.21
  1.4 0.7 slice.22
  2.0 0.7 slice.23
  2.7 1.2 %broadcast_in_dim.15.bin_ref = f32[1,384]{1,0:T(1,128)} reshape(f32[384]{0:T(512)} %param.15) | data formatting | bytes 3072 | tf_op jit(solution)/shard_map/broadcast_in_dim | solution.py:261
  4.0 1.3 %broadcast_in_dim.16.gin_ref = f32[1,384]{1,0:T(1,128)} reshape(f32[384]{0:T(512)} %param.16) | data formatting | bytes 3072 | tf_op jit(solution)/shard_map/broadcast_in_dim | solution.py:261
  5.2 0.7 tile.2
  5.9 0.7 broadcast_in_dim_tile.3.bf_ref
  6.6 0.8 concatenate.13
  7.4 0.6 broadcast_in_dim.19.gl_ref
  8.0 0.8 concatenate.12
  8.8 0.6 broadcast_in_dim.18.bl_ref
  9.4 1.3 %broadcast_in_dim.17.btime_ref = f32[1,768]{1,0:T(1,128)} reshape(f32[768]{0:T(1024)} %param.18) | data formatting | bytes 6144 | tf_op jit(solution)/shard_map/broadcast_in_dim | solution.py:261
  10.7 1.3 %copy-done.2 = bf16[3,3,384,192]{2,3,1,0:T(8,128)(2,1)S(1)} copy-done((bf16[3,3,384,192]{2,3,1,0:T(8,128)(2,1)S(1)}, bf16[3,3,384,192]{2,3,1,0:T(8,128)(2,1)}, u32[]{:S(2)}) %copy-start.2) | copy-done | bytes 1327128
  12.0 1.0 %copy-done.4 = bf16[3,3,192,96]{3,2,1,0:T(8,128)(2,1)S(1)} copy-done((bf16[3,3,192,96]{3,2,1,0:T(8,128)(2,1)S(1)}, bf16[3,3,192,96]{3,2,1,0:T(8,128)(2,1)}, u32[]{:S(2)}) %copy-start.4) | copy-done | bytes 331800
  13.1 1.0 %copy-done.5 = bf16[3,3,3,16,384]{4,3,2,1,0:T(8,128)(2,1)S(1)} copy-done((bf16[3,3,3,16,384]{4,3,2,1,0:T(8,128)(2,1)S(1)}, bf16[3,3,3,16,384]{4,3,2,1,0:T(8,128)(2,1)}, u32[]{:S(2)}) %copy-start.5) | copy-done | bytes 331800
  14.0 0.8 copy-done.7
  14.8 0.7 copy-done.8
  15.4 26.0 %exchange.1 = (bf16[3,256,128]{2,1,0:T(8,128)(2,1)S(1)}, bf16[768,768]{1,0:T(8,128)(2,1)S(1)}, bf16[1536,768]{1,0:T(8,128)(2,1)S(1)}, bf16[4,768,512]{2,1,0:T(8,128)(2,1)S(1)}) custom-call(bf16[128,128]{1,0:T(8,128)(2,1)S(1)} %copy-done.7, s32[128]{0:T(128)S(1)} %copy-done.8, bf16[3,3,3,16,384]{4,3,2,1,0:T(8,128)(2,1)S(1)} %copy-done.5, ...), custom_call_target="tpu_custom_call" | custom-call | tf_op jit(solution)/shard_map/exchange/pallas_call | solution.py:411
  41.5 1.6 %copy-done = bf16[4,768,512]{2,1,0:T(8,128)(2,1)} copy-done((bf16[4,768,512]{2,1,0:T(8,128)(2,1)}, bf16[4,768,512]{2,1,0:T(8,128)(2,1)S(1)}, u32[]{:S(2)}) %copy-start) | copy-done | bytes 3145752
  43.1 1.5 %copy-done.1 = bf16[1536,768]{1,0:T(8,128)(2,1)} copy-done((bf16[1536,768]{1,0:T(8,128)(2,1)}, bf16[1536,768]{1,0:T(8,128)(2,1)S(1)}, u32[]{:S(2)}) %copy-start.1) | copy-done | bytes 2359320
  44.6 1.0 %copy-done.3 = bf16[768,768]{1,0:T(8,128)(2,1)} copy-done((bf16[768,768]{1,0:T(8,128)(2,1)}, bf16[768,768]{1,0:T(8,128)(2,1)S(1)}, u32[]{:S(2)}) %copy-start.3) | copy-done | bytes 1179672
  45.7 0.7 copy-done.6
  46.4 40.3 %decode.1 = bf16[4,16,49152]{2,1,0:T(8,128)(2,1)} custom-call(bf16[3,256,128]{2,1,0:T(8,128)(2,1)} %copy-done.6, bf16[768,768]{1,0:T(8,128)(2,1)} %copy-done.3, f32[1,384]{1,0:T(1,128)} %broadcast_in_dim.15.bin_ref, f32[1,384]{1,0:T(1,128)} %broadcast_in_dim.16.gin_ref, bf16[1152,768]{1,0:T(8,128)(2,1)} %bitcast.3, f32[1,768]{1,0:T(1,128)} %broadcast_in_dim.17.btime_ref, ...), custom_call_target="tpu_custom_call" | custom-call | tf_op jit(solution)/shard_map/decode/pallas_call | solution.py:268
  (9 shorter events, 0.0 us)
Async XLA Ops:
  10.7 1.3 %copy-start.2 = (bf16[3,3,384,192]{2,3,1,0:T(8,128)(2,1)S(1)}, bf16[3,3,384,192]{2,3,1,0:T(8,128)(2,1)}, u32[]{:S(2)}) copy-start(bf16[3,3,384,192]{2,3,1,0:T(8,128)(2,1)} %param.19) | copy-start | bytes 3981316
  12.0 1.0 %copy-start.4 = (bf16[3,3,192,96]{3,2,1,0:T(8,128)(2,1)S(1)}, bf16[3,3,192,96]{3,2,1,0:T(8,128)(2,1)}, u32[]{:S(2)}) copy-start(bf16[3,3,192,96]{3,2,1,0:T(8,128)(2,1)} %wfinal_hbm.1) | copy-start | bytes 995332
  13.1 1.0 %copy-start.5 = (bf16[3,3,3,16,384]{4,3,2,1,0:T(8,128)(2,1)S(1)}, bf16[3,3,3,16,384]{4,3,2,1,0:T(8,128)(2,1)}, u32[]{:S(2)}) copy-start(bf16[3,3,3,16,384]{4,3,2,1,0:T(8,128)(2,1)} %win_hbm.1) | copy-start | bytes 995332
  14.0 0.8 copy-start.7
  14.8 0.7 copy-start.8
  41.5 1.6 %copy-start = (bf16[4,768,512]{2,1,0:T(8,128)(2,1)}, bf16[4,768,512]{2,1,0:T(8,128)(2,1)S(1)}, u32[]{:S(2)}) copy-start(bf16[4,768,512]{2,1,0:T(8,128)(2,1)S(1)} %get-tuple-element.12.wf_ref) | copy-start | bytes 9437188
  43.1 1.5 %copy-start.1 = (bf16[1536,768]{1,0:T(8,128)(2,1)}, bf16[1536,768]{1,0:T(8,128)(2,1)S(1)}, u32[]{:S(2)}) copy-start(bf16[1536,768]{1,0:T(8,128)(2,1)S(1)} %get-tuple-element.11.wl_ref) | copy-start | bytes 7077892
  44.6 1.1 %copy-start.3 = (bf16[768,768]{1,0:T(8,128)(2,1)}, bf16[768,768]{1,0:T(8,128)(2,1)S(1)}, u32[]{:S(2)}) copy-start(bf16[768,768]{1,0:T(8,128)(2,1)S(1)} %get-tuple-element.10.band_ref) | copy-start | bytes 3538948
  45.7 0.7 copy-start.6

commit v2 on v1

--- a/solution.py
+++ b/solution.py
@@ -8,8 +8,9 @@
 from jax.sharding import PartitionSpec as P
 
 BF16, F32 = jnp.bfloat16, jnp.float32
-XB = 16
-SC = 4
+XB = 32
+SC = 8
+VMEM_LIMIT = 60 * 1024 * 1024
 
 
 def silu(n):
@@ -82,7 +83,7 @@
                             final_ref[2 * jpar + xpar, slot : slot + 64, lane : lane + 128] = tile.astype(BF16)
 
 
-def front(blocks_ref, band_ref, bin_ref, gin_ref, wtime_ref, btime_ref, grid_ref, dbl_ref):
+def front(blocks_ref, band_ref, bin_ref, gin_ref, wtime_ref, btime_ref, grid_ref, dbl_ref, loads):
     row, frame = lax.axis_index("rows"), lax.axis_index("frames")
     top, bottom = row == 0, row == lax.axis_size("rows") - 1
     out_row = lax.broadcasted_iota(jnp.int32, (256, 256), 0)
@@ -111,6 +112,10 @@
     for v in range(3):
         dbl_ref[v, 0:1] = edge_col
         dbl_ref[v, dbl_ref.shape[1] - 1 :] = edge_col
+
+    loads[0].wait()
+    loads[1].wait()
+    b_in, g_in, b_time = (v[...].reshape(1, -1) for v in (bin_ref, gin_ref, btime_ref))
 
     def chunk(step, carry):
         s0 = step * SC
@@ -137,9 +142,9 @@
         hidden = jnp.dot(patch.reshape(4 * SC * 32, 768), band_ref[...], preferred_element_type=F32)
         halves = []
         for pp in range(2):
-            h = hidden[:, 384 * pp : 384 * (pp + 1)] + bin_ref[...]
+            h = hidden[:, 384 * pp : 384 * (pp + 1)] + b_in
             mean = jnp.sum(h * h, axis=-1, keepdims=True) * (1.0 / 384)
-            v = silu(h * lax.rsqrt(mean + 1e-6) * gin_ref[...])
+            v = silu(h * lax.rsqrt(mean + 1e-6) * g_in)
             halves.append(v.reshape(4, SC * 4, 8, 384))
         feats = jnp.stack(halves, axis=2)
         t_in = lax.broadcasted_iota(jnp.int32, (4, 1, 1, 1, 1), 0)
@@ -147,7 +152,7 @@
         feats = feats.reshape(4, SC * 64, 384).astype(BF16)
         hist = jnp.concatenate([feats[k : k + 2] for k in range(3)], axis=-1)
         acc = jnp.dot(hist.reshape(2 * SC * 64, 1152), wtime_ref[...], preferred_element_type=F32)
-        acc = acc + btime_ref[...]
+        acc = acc + b_time
         acc = acc.reshape(2, SC * 8, 8, 768)
         for v in range(3):
             both = []
@@ -237,48 +242,59 @@
                 out_ref[2 * t + j, :, 128 * n : 128 * (n + 1)] = rows_ref[n, base : base + 16, :].astype(BF16)
 
 
+def spread(half):
+    wide, narrow = half[:, :128], half[:, 128:]
+    return jnp.concatenate([wide, narrow, narrow, wide] * 2, axis=-1)
+
+
 def decode_kernel(
-    blocks_ref, band_ref, bin_ref, gin_ref, wtime_ref, btime_ref, wl_ref, bl_ref, gl_ref, wf_ref, bf_ref,
-    out_ref, grid_ref, dbl_ref, rows_ref,
+    blocks_ref, band_hbm, bin_ref, gin_ref, wtime_hbm, btime_ref, lift_hbm, blift_ref, glift_ref, final_hbm, bfinal_ref,
+    out_ref, grid_ref, dbl_ref, rows_ref, band_ref, wtime_ref, wl_ref, wf_ref, bl_ref, gl_ref, bf_ref, load_sem,
 ):
     step = pl.program_id(0)
 
     @pl.when(step == 0)
     def _():
-        front(blocks_ref, band_ref, bin_ref, gin_ref, wtime_ref, btime_ref, grid_ref, dbl_ref)
+        loads = [
+            pltpu.make_async_copy(src, dst, load_sem.at[n])
+            for n, (src, dst) in enumerate(
+                ((band_hbm, band_ref), (wtime_hbm, wtime_ref), (lift_hbm, wl_ref), (final_hbm, wf_ref))
+            )
+        ]
+        for copy in loads:
+            copy.start()
+        bl_ref[...] = spread(blift_ref[...].reshape(1, -1))
+        gl_ref[...] = spread(glift_ref[...].reshape(1, -1))
+        bf_ref[...] = jnp.concatenate([bfinal_ref[...].reshape(1, -1)] * 4, axis=-1)
+        front(blocks_ref, band_ref, bin_ref, gin_ref, wtime_ref, btime_ref, grid_ref, dbl_ref, loads)
+        loads[2].wait()
+        loads[3].wait()
 
     back(step, dbl_ref, wl_ref, bl_ref, gl_ref, wf_ref, bf_ref, out_ref, rows_ref)
-
-
-def lanes_of_phases(v):
-    half = jnp.concatenate([v[:128], v[128:], v[128:], v[:128]])
-    return jnp.concatenate([half, half])[None]
 
 
 def decode(blocks, band, wl, wf, b_in, gain_in, w_time, b_time, b_lift, gain_lift, b_final):
     width = 128
-    args = (
-        blocks, band, b_in[None], gain_in[None], w_time.reshape(1152, 768), b_time[None],
-        wl, lanes_of_phases(b_lift), lanes_of_phases(gain_lift), wf, jnp.tile(b_final, 4)[None],
-    )
-
-    def whole(a):
-        return pl.BlockSpec(a.shape, lambda i: (0,) * a.ndim, pipeline_mode=pl.Buffered(1))
-
+    vmem, hbm = pl.BlockSpec(memory_space=pltpu.VMEM), pl.BlockSpec(memory_space=pltpu.HBM)
+    w_time = w_time.reshape(-1, w_time.shape[-1])
+    weights = (band, w_time, wl, wf)
     return pl.pallas_call(
         decode_kernel,
         grid=(width // XB,),
-        in_specs=[whole(a) for a in args],
+        in_specs=[vmem, hbm, vmem, vmem, hbm, vmem, hbm, vmem, vmem, hbm, vmem],
         out_specs=pl.BlockSpec((4, 16, XB * 384), lambda i: (0, 0, i)),
         out_shape=jax.ShapeDtypeStruct((4, 16, width * 384), BF16),
         scratch_shapes=[
             pltpu.VMEM((6, 18, 8, 128), F32),
             pltpu.VMEM((3, width + 2, 16, 384), BF16),
             pltpu.VMEM((XB * 3, 64, 128), F32),
-        ],
-        compiler_params=pltpu.CompilerParams(vmem_limit_bytes=56 * 1024 * 1024),
+        ]
+        + [pltpu.VMEM(w.shape, BF16) for w in weights]
+        + [pltpu.VMEM((1, 768), F32), pltpu.VMEM((1, 768), F32), pltpu.VMEM((1, 384), F32)]
+        + [pltpu.SemaphoreType.DMA((4,))],
+        compiler_params=pltpu.CompilerParams(vmem_limit_bytes=VMEM_LIMIT),
         name="decode",
-    )(*args)
+    )(blocks, band, b_in, gain_in, w_time, b_time, wl, b_lift, gain_lift, wf, b_final)
 
 
 def exchange_kernel(
@@ -426,7 +442,7 @@
         + [pltpu.VMEM(shape, BF16) for shape in made]
         + [dma((3,)), dma((3,)), dma((rows,)), dma((rows,)), dma((frames,)), dma((frames,)), dma((8,)), dma((8,))],
         compiler_params=pltpu.CompilerParams(
-            collective_id=0, has_side_effects=True, vmem_limit_bytes=40 * 1024 * 1024
+            collective_id=0, has_side_effects=True, vmem_limit_bytes=VMEM_LIMIT
         ),
         name="exchange",
     )(latents, tile_slot, *weights)

time: 87.2 us -> 64.2 us (0.74)
  local copies, waits for them, and re-layouts: 20.3 us -> 0 us
  Pallas kernels: 66.4 us -> 64 us
    unnamed x18 -> x0, local copies, waits for them, and re-layouts: 9.57 us -> none
    broadcast_in_dim x5 -> x0, local copies, waits for them, and re-layouts: 5 us -> none  [the longest x1 1.28 us: decode(): b_time[None]]
    pallas_call x1, Pallas kernels: 40.3 us -> 37 us  [decode(): pl.pallas_call(decode_kernel, grid=(width // XB,), in_specs=[vmem, hbm, v...]
    slice x4 -> x0, local copies, waits for them, and re-layouts: 2.72 us -> none  [lanes_of_phases(): half = jnp.concatenate([v[:128], v[128:], v[128:], v[:128]])]
    concatenate x2 -> x0, local copies, waits for them, and re-layouts: 1.66 us -> none  [lanes_of_phases(): return jnp.concatenate([half, half])[None]]
    another operation x2 -> x0, local copies, waits for them, and re-layouts: 1.33 us -> none  [decode(): jnp.tile(b_final, 4)[None]]
    pallas_call x1, Pallas kernels: 26 us -> 26.9 us  [exchange(): pl.pallas_call(functools.partial(exchange_kernel, rows, frames), in_specs...]
where the time goes in v2:
time: 64.2 us; the launch traced here: 64 us
  Pallas kernels  64 us (100%)
    pallas_call x1, Pallas kernels, decode(): pl.pallas_call(decode_kernel, grid=(width // XB,), in_specs=[vmem, hbm, v...  37 us
    pallas_call x1, Pallas kernels, exchange(): pl.pallas_call(functools.partial(exchange_kernel, rows, frames), in_specs...  26.9 us

profile of v2, /device:TPU:1, one launch (start us, length us, event | category | flops | bytes accessed | tf_op | source)
XLA Modules:
  0.0 64.0 jit_solution(10960054525628316568)
XLA Ops:
  0.0 26.9 %exchange.1 = (bf16[3,256,128]{2,1,0:T(8,128)(2,1)}, bf16[768,768]{1,0:T(8,128)(2,1)}, bf16[1536,768]{1,0:T(8,128)(2,1)}, bf16[4,768,512]{2,1,0:T(8,128)(2,1)}) custom-call(bf16[128,128]{1,0:T(8,128)(2,1)} %lat_ref.1, s32[128]{0:T(128)} %slot_ref.1, bf16[3,3,3,16,384]{4,3,2,1,0:T(8,128)(2,1)} %win_hbm.1, bf16[3,3,192,384]{3,2,1,0:T(8,128)(2,1)} %bitcast.3, ...), custom_call_target="tpu_custom_call" | custom-call | tf_op jit(solution)/shard_map/exchange/pallas_call | solution.py:427
  26.9 37.0 %decode.1 = bf16[4,16,49152]{2,1,0:T(8,128)(2,1)} custom-call(bf16[3,256,128]{2,1,0:T(8,128)(2,1)} %get-tuple-element.9.blocks_ref, bf16[768,768]{1,0:T(8,128)(2,1)} %get-tuple-element.10.band_hbm, f32[384]{0:T(512)} %bin_ref.1, f32[384]{0:T(512)} %gin_ref.1, bf16[1152,768]{1,0:T(8,128)(2,1)} %bitcast.2, f32[768]{0:T(1024)} %btime_ref.1, ...), custom_call_target="tpu_custom_call" | custom-call | tf_op jit(solution)/shard_map/decode/pallas_call | solution.py:281

commit v3 on v2

--- a/solution.py
+++ b/solution.py
@@ -8,13 +8,13 @@
 from jax.sharding import PartitionSpec as P
 
 BF16, F32 = jnp.bfloat16, jnp.float32
-XB = 32
+XB = 64
+SUB = 32
 SC = 8
 VMEM_LIMIT = 60 * 1024 * 1024
 
 
-def silu(n):
-    half = 0.5 * n
+def silu_of_half(half):
     return half + half * jnp.tanh(half)
 
 
@@ -83,7 +83,7 @@
                             final_ref[2 * jpar + xpar, slot : slot + 64, lane : lane + 128] = tile.astype(BF16)
 
 
-def front(blocks_ref, band_ref, bin_ref, gin_ref, wtime_ref, btime_ref, grid_ref, dbl_ref, loads):
+def front(block_refs, band_ref, bin_ref, gin_ref, wtime_ref, btime_ref, grid_ref, dbl_ref, loads):
     row, frame = lax.axis_index("rows"), lax.axis_index("frames")
     top, bottom = row == 0, row == lax.axis_size("rows") - 1
     out_row = lax.broadcasted_iota(jnp.int32, (256, 256), 0)
@@ -103,25 +103,26 @@
     grid_ref[:, 17:18] = zero_col
     for part in range(3):
         select = jnp.where(jnp.logical_and(chosen, frame + part >= 2), 1.0, 0.0).astype(BF16)
-        picked = jnp.dot(select, blocks_ref[part], preferred_element_type=F32)
+        cells = jnp.concatenate([ref[part].reshape(-1, 128) for ref in block_refs], axis=0)
+        picked = jnp.dot(select, cells, preferred_element_type=F32)
         grid_ref[2 * part : 2 * part + 2, 1:17] = picked.reshape(2, 16, 8, 128)
 
     lane = lax.broadcasted_iota(jnp.int32, (1, 1, 1, 128), 3)
     sub = lax.broadcasted_iota(jnp.int32, (1, 1, 8, 1), 2)
-    edge_col = jnp.zeros((1, 16, 384), BF16)
-    for v in range(3):
-        dbl_ref[v, 0:1] = edge_col
-        dbl_ref[v, dbl_ref.shape[1] - 1 :] = edge_col
+    edge_col = jnp.zeros((3, 1, 32, 128), F32)
+    dbl_ref[:, 0:1] = edge_col
+    dbl_ref[:, dbl_ref.shape[1] - 1 :] = edge_col
 
     loads[0].wait()
     loads[1].wait()
     b_in, g_in, b_time = (v[...].reshape(1, -1) for v in (bin_ref, gin_ref, btime_ref))
+    g_in = 0.5 * g_in
 
     def chunk(step, carry):
         s0 = step * SC
         cells = grid_ref[:, pl.ds(s0, SC + 2)]
         flat = cells.reshape(6 * (SC + 2), 8, 128)
-        turned = [pltpu.roll(flat, 1, 1), flat, pltpu.roll(flat, 7, 1)]
+        turned = [flat, pltpu.roll(flat, 7, 1), pltpu.roll(flat, 6, 1)]
         pieces = []
         for q in range(4):
             shift = (16 - 32 * q) % 128
@@ -144,69 +145,89 @@
         for pp in range(2):
             h = hidden[:, 384 * pp : 384 * (pp + 1)] + b_in
             mean = jnp.sum(h * h, axis=-1, keepdims=True) * (1.0 / 384)
-            v = silu(h * lax.rsqrt(mean + 1e-6) * g_in)
+            v = silu_of_half(h * lax.rsqrt(mean + 1e-6) * g_in)
             halves.append(v.reshape(4, SC * 4, 8, 384))
         feats = jnp.stack(halves, axis=2)
-        t_in = lax.broadcasted_iota(jnp.int32, (4, 1, 1, 1, 1), 0)
-        feats = jnp.where(t_in + 2 * frame >= 2, feats, 0.0)
+        feats = jnp.concatenate([jnp.where(frame > 0, feats[:2], 0.0), feats[2:]], axis=0)
         feats = feats.reshape(4, SC * 64, 384).astype(BF16)
         hist = jnp.concatenate([feats[k : k + 2] for k in range(3)], axis=-1)
         acc = jnp.dot(hist.reshape(2 * SC * 64, 1152), wtime_ref[...], preferred_element_type=F32)
         acc = acc + b_time
         acc = acc.reshape(2, SC * 8, 8, 768)
-        for v in range(3):
-            both = []
+        for t in range(2):
             for j in range(2):
-                a0 = pltpu.roll(acc[0, :, :, 384 * j : 384 * (j + 1)], 7 - v, 1)
-                a1 = pltpu.roll(acc[1, :, :, 384 * j : 384 * (j + 1)], 3 - v, 1)
-                both.append(jnp.where(sub[0] < 4, a0, a1))
-            full = jnp.concatenate(both, axis=1)
-            group = lax.broadcasted_iota(jnp.int32, (1, 16, 1), 1) % 4
-            if v == 0:
-                full = jnp.where(jnp.logical_and(top, group == 0), 0.0, full)
-            if v == 2:
-                full = jnp.where(jnp.logical_and(bottom, group == 3), 0.0, full)
-            dbl_ref[v, pl.ds(8 * s0 + 1, SC * 8)] = full.astype(BF16)
+                for k in range(3):
+                    lanes = acc[t, :, :, 384 * j + 128 * k : 384 * j + 128 * (k + 1)]
+                    dbl_ref[k, pl.ds(8 * s0 + 1, SC * 8), pl.ds(2 * j + t, 8, stride=4), :] = lanes
         return carry
 
     lax.fori_loop(0, 16 // SC, chunk, 0)
 
-
-def back(step, dbl_ref, wl_ref, bl_ref, gl_ref, wf_ref, bf_ref, out_ref, rows_ref):
+    @pl.when(top)
+    def _():
+        dbl_ref[:, :, 0:4, :] = jnp.zeros((3, dbl_ref.shape[1], 4, 128), F32)
+
+    @pl.when(bottom)
+    def _():
+        dbl_ref[:, :, 20:24, :] = jnp.zeros((3, dbl_ref.shape[1], 4, 128), F32)
+
+
+def back(step, sub, dbl_ref, wl_ref, bl_ref, gl_ref, wf_ref, bf_ref, out_ref, rows_ref, sec_ref):
     row = lax.axis_index("rows")
     top, bottom = row == 0, row == lax.axis_size("rows") - 1
     width = dbl_ref.shape[1] - 2
-    x0 = step * XB
-    count = XB + 1
+    x0 = step * XB + sub
+    count = SUB + 1
     lane = lax.broadcasted_iota(jnp.int32, (1, 1, 128), 2)
     low = lane < 64
-    d_m, d_0, d_p = (dbl_ref[v, pl.ds(x0, XB + 2)] for v in range(3))
-    group = lax.broadcasted_iota(jnp.int32, (1, 16, 1), 1) % 4
-    col = lax.broadcasted_iota(jnp.int32, (count, 1, 1), 0) + (x0 - 1)
-
-    def lift(upper, lower, drop):
-        patch = jnp.concatenate([upper[:-1], upper[1:], lower[:-1], lower[1:]], axis=-1)
-        acc = jnp.dot(patch.reshape(count * 16, -1), wl_ref[...], preferred_element_type=F32)
-        acc = acc.reshape(count, 16, 768) + bl_ref[...]
+    half = lax.broadcasted_iota(jnp.int32, (1, 8, 1), 1) < 4
+
+    patch = []
+    for ty in range(2):
+        tiles = [dbl_ref[k, pl.ds(x0, count + 1), 4 * ty : 4 * ty + 24, :] for k in range(3)]
+        patch += [v[tx : tx + count].reshape(count * 24, 128).astype(BF16) for tx in range(2) for v in tiles]
+    acc = jnp.dot(jnp.concatenate(patch, axis=-1), wl_ref[...], preferred_element_type=F32)
+    acc = acc.reshape(count, 24, 768) + bl_ref[...]
+    first_rows = lax.broadcasted_iota(jnp.int32, (1, 8, 1), 1) < 4
+    above, below = jnp.logical_and(first_rows, top), jnp.logical_and(first_rows, bottom)
+
+    def keep(n, v):
+        px, k = n // 3, n % 3
+        for g in range(3):
+            part = v[:, 8 * g : 8 * (g + 1)]
+            if g == 0 and k < 2:
+                part = jnp.where(above if k == 0 else jnp.logical_and(above, low), 0.0, part)
+            if g == 2 and k > 0:
+                part = jnp.where(below if k == 2 else jnp.logical_and(below, jnp.logical_not(low)), 0.0, part)
+            rows = slice(16 + 8 * g, 24 + 8 * g)
+            if px == 0:
+                sec_ref[sub // SUB, n, 0:1, rows, :] = jnp.where(x0 == 0, 0.0, part[0:1])
+                sec_ref[sub // SUB, n, 1:count, rows, :] = part[1:]
+            else:
+                sec_ref[sub // SUB, n, 0 : count - 1, rows, :] = part[:-1]
+                sec_ref[sub // SUB, n, count - 1 : count, rows, :] = jnp.where(x0 == width - SUB, 0.0, part[-1:])
+
+    for px in range(2):
+        tiles = [acc[..., 384 * px + 128 * k : 384 * px + 128 * (k + 1)] for k in range(3)]
+        sq = [v * v for v in tiles]
+        s0 = jnp.sum(sq[0] + jnp.where(low, sq[1], 0.0), axis=-1, keepdims=True)
+        s1 = jnp.sum(sq[2] + jnp.where(low, 0.0, sq[1]), axis=-1, keepdims=True)
+        f0 = lax.rsqrt(s0 * (1.0 / 192) + 1e-6)
+        f1 = lax.rsqrt(s1 * (1.0 / 192) + 1e-6)
+        for k, f in enumerate((f0, jnp.where(low, f0, f1), f1)):
+            v = silu_of_half(tiles[k] * f * gl_ref[:, 384 * px + 128 * k : 384 * px + 128 * (k + 1)])
+            keep(3 * px + k, v)
+
+    def window(k, first):
         out = []
-        for px in range(2):
-            tiles = [acc[..., 384 * px + 128 * k : 384 * px + 128 * (k + 1)] for k in range(3)]
-            sq = [v * v for v in tiles]
-            s0 = jnp.sum(sq[0] + jnp.where(low, sq[1], 0.0), axis=-1, keepdims=True)
-            s1 = jnp.sum(sq[2] + jnp.where(low, 0.0, sq[1]), axis=-1, keepdims=True)
-            f0 = lax.rsqrt(s0 * (1.0 / 192) + 1e-6)
-            f1 = lax.rsqrt(s1 * (1.0 / 192) + 1e-6)
-            inside = (col >= 0) if px == 0 else (col < width - 1)
-            for k, f in enumerate((f0, jnp.where(low, f0, f1), f1)):
-                v = silu(tiles[k] * f * gl_ref[:, 384 * px + 128 * k : 384 * px + 128 * (k + 1)])
-                keep = inside if drop[k] is None else jnp.logical_and(inside, jnp.logical_not(drop[k]))
-                out.append(jnp.where(keep, v, 0.0).astype(BF16))
-        return out
-
-    above = jnp.logical_and(group == 0, top)
-    below = jnp.logical_and(group == 3, bottom)
-    s_m = lift(d_m, d_0, (above, jnp.logical_and(above, low), None))
-    s_p = lift(d_0, d_p, (None, jnp.logical_and(below, jnp.logical_not(low)), below))
+        for h in range(2):
+            lo = sec_ref[sub // SUB, k, :, pl.ds(16 + 4 * first + 2 * h, 8, stride=4), :]
+            hi = sec_ref[sub // SUB, k, :, pl.ds(4 * first + 2 * h + 1, 8, stride=4), :]
+            out.append(jnp.where(half, lo, hi))
+        return jnp.concatenate(out, axis=1).astype(BF16)
+
+    s_m = [window(k, 0) for k in range(6)]
+    s_p = [window(k, 1) for k in range(6)]
     s_e = []
     for px in range(2):
         s_e += [s_p[3 * px], jnp.where(low, s_p[3 * px + 1], s_m[3 * px + 1]), s_m[3 * px + 2]]
@@ -215,7 +236,7 @@
         return jnp.concatenate(tiles, axis=-1).reshape(count * 16, 768)
 
     def even(tiles):
-        return jnp.concatenate([v[1:] for v in tiles[:3]] + [v[:-1] for v in tiles[3:]], axis=-1).reshape(XB * 16, 768)
+        return jnp.concatenate([v[1:] for v in tiles[:3]] + [v[:-1] for v in tiles[3:]], axis=-1).reshape(SUB * 16, 768)
 
     def mul(lhs, kind, lo, hi):
         return jnp.dot(lhs, wf_ref[kind, :, lo:hi], preferred_element_type=F32).reshape(-1, 16, hi - lo)
@@ -233,12 +254,12 @@
         t2 = jnp.where(lane < 32, e[..., :128], o[1:, :, :128])
         for k, t in enumerate((t0, t1, t2)):
             t = t + bf_ref[:, 128 * k : 128 * (k + 1)]
-            for u in range(XB):
-                rows_ref[3 * u + k, pl.ds(a, 16, stride=4), :] = t[u]
+            for u in range(SUB):
+                rows_ref[3 * (sub + u) + k, pl.ds(a, 16, stride=4), :] = t[u]
     for j in range(2):
         for t in range(2):
             base = 16 * (2 * j + t)
-            for n in range(3 * XB):
+            for n in range(3 * sub, 3 * (sub + SUB)):
                 out_ref[2 * t + j, :, 128 * n : 128 * (n + 1)] = rows_ref[n, base : base + 16, :].astype(BF16)
 
 
@@ -248,8 +269,8 @@
 
 
 def decode_kernel(
-    blocks_ref, band_hbm, bin_ref, gin_ref, wtime_hbm, btime_ref, lift_hbm, blift_ref, glift_ref, final_hbm, bfinal_ref,
-    out_ref, grid_ref, dbl_ref, rows_ref, band_ref, wtime_ref, wl_ref, wf_ref, bl_ref, gl_ref, bf_ref, load_sem,
+    above_ref, own_ref, below_ref, band_hbm, bin_ref, gin_ref, wtime_hbm, btime_ref, lift_hbm, blift_ref, glift_ref, final_hbm, bfinal_ref,
+    out_ref, grid_ref, dbl_ref, rows_ref, sec_ref, band_ref, wtime_ref, wl_ref, wf_ref, bl_ref, gl_ref, bf_ref, load_sem,
 ):
     step = pl.program_id(0)
 
@@ -264,16 +285,17 @@
         for copy in loads:
             copy.start()
         bl_ref[...] = spread(blift_ref[...].reshape(1, -1))
-        gl_ref[...] = spread(glift_ref[...].reshape(1, -1))
+        gl_ref[...] = 0.5 * spread(glift_ref[...].reshape(1, -1))
         bf_ref[...] = jnp.concatenate([bfinal_ref[...].reshape(1, -1)] * 4, axis=-1)
-        front(blocks_ref, band_ref, bin_ref, gin_ref, wtime_ref, btime_ref, grid_ref, dbl_ref, loads)
+        front((above_ref, own_ref, below_ref), band_ref, bin_ref, gin_ref, wtime_ref, btime_ref, grid_ref, dbl_ref, loads)
         loads[2].wait()
         loads[3].wait()
 
-    back(step, dbl_ref, wl_ref, bl_ref, gl_ref, wf_ref, bf_ref, out_ref, rows_ref)
-
-
-def decode(blocks, band, wl, wf, b_in, gain_in, w_time, b_time, b_lift, gain_lift, b_final):
+    for sub in range(0, XB, SUB):
+        back(step, sub, dbl_ref, wl_ref, bl_ref, gl_ref, wf_ref, bf_ref, out_ref, rows_ref, sec_ref)
+
+
+def decode(above, own, below, band, wl, wf, b_in, gain_in, w_time, b_time, b_lift, gain_lift, b_final):
     width = 128
     vmem, hbm = pl.BlockSpec(memory_space=pltpu.VMEM), pl.BlockSpec(memory_space=pltpu.HBM)
     w_time = w_time.reshape(-1, w_time.shape[-1])
@@ -281,36 +303,46 @@
     return pl.pallas_call(
         decode_kernel,
         grid=(width // XB,),
-        in_specs=[vmem, hbm, vmem, vmem, hbm, vmem, hbm, vmem, vmem, hbm, vmem],
+        in_specs=[vmem, vmem, vmem, hbm, vmem, vmem, hbm, vmem, hbm, vmem, vmem, hbm, vmem],
         out_specs=pl.BlockSpec((4, 16, XB * 384), lambda i: (0, 0, i)),
         out_shape=jax.ShapeDtypeStruct((4, 16, width * 384), BF16),
         scratch_shapes=[
             pltpu.VMEM((6, 18, 8, 128), F32),
-            pltpu.VMEM((3, width + 2, 16, 384), BF16),
+            pltpu.VMEM((3, width + 2, 32, 128), F32),
             pltpu.VMEM((XB * 3, 64, 128), F32),
+            pltpu.VMEM((XB // SUB, 6, SUB + 1, 56, 128), F32),
         ]
         + [pltpu.VMEM(w.shape, BF16) for w in weights]
         + [pltpu.VMEM((1, 768), F32), pltpu.VMEM((1, 768), F32), pltpu.VMEM((1, 384), F32)]
         + [pltpu.SemaphoreType.DMA((4,))],
         compiler_params=pltpu.CompilerParams(vmem_limit_bytes=VMEM_LIMIT),
         name="decode",
-    )(blocks, band, b_in, gain_in, w_time, b_time, wl, b_lift, gain_lift, wf, b_final)
+    )(above, own, below, band, b_in, gain_in, w_time, b_time, wl, b_lift, gain_lift, wf, b_final)
+
+
+def far_first(count):
+    return sorted(range(1, count), key=lambda k: -min(k, count - k))
 
 
 def exchange_kernel(
     rows, frames,
-    lat_ref, slot_ref, win_hbm, wlift_hbm, wfinal_hbm,
-    blocks_ref, band_hbm, lift_hbm, final_hbm,
-    send1, recv1, send2, recv2, above, own, below, win_ref, wlift_ref, wfinal_ref, band_ref, lift_ref, final_ref,
+    lat_hbm, slot_hbm, win_hbm, wlift_hbm, wfinal_hbm,
+    above, own, below, band_hbm, lift_hbm, final_hbm,
+    lat_ref, slot_ref, send1, recv1, send2, recv2, block, win_ref, wlift_ref, wfinal_ref, band_ref, lift_ref, final_ref,
     load_sem, store_sem, send_sem1, recv_sem1, send_sem2, recv_sem2, send_sem3, recv_sem3,
 ):
     r, f = lax.axis_index("rows"), lax.axis_index("frames")
     loads = [
         pltpu.make_async_copy(src, dst, load_sem.at[n])
-        for n, (src, dst) in enumerate(((win_hbm, win_ref), (wlift_hbm, wlift_ref), (wfinal_hbm, wfinal_ref)))
+        for n, (src, dst) in enumerate(
+            (
+                (win_hbm, win_ref), (wlift_hbm, wlift_ref), (wfinal_hbm, wfinal_ref),
+                (lat_hbm, lat_ref), (slot_hbm, slot_ref),
+            )
+        )
     ]
-    for copy in loads:
-        copy.start()
+    loads[4].start()
+    loads[3].start()
 
     def at(dr, df):
         return {"rows": lax.rem(r + dr + rows, rows), "frames": lax.rem(f + df + frames, frames)}
@@ -321,6 +353,11 @@
     sources = [(k, 0) for k in range(1, rows)] + [(0, k) for k in range(1, frames)] + [(-dr, -df) for dr, df in far]
     for dr, df in sources:
         pl.semaphore_signal(barrier, inc=1, device_id=at(dr, df), device_id_type=pl.DeviceIdType.MESH)
+
+    for copy in loads[:3]:
+        copy.start()
+    loads[4].wait()
+    loads[3].wait()
 
     slots, width = lat_ref.shape
     across = jnp.broadcast_to(slot_ref[...].reshape(1, slots), (slots, slots))
@@ -346,7 +383,7 @@
         )
 
     first = []
-    for k in range(1, rows):
+    for k in far_first(rows):
         peer, source = lax.rem(r + k, rows), lax.rem(r - k + rows, rows)
         out = remote(send1.at[peer], recv1.at[r], send_sem1.at[k], recv_sem1.at[k], k, 0)
         out.start()
@@ -368,7 +405,7 @@
     send2[...] = moved.astype(BF16).reshape(send2.shape)
     recv2[f] = send2[f]
     second = []
-    for k in range(1, frames):
+    for k in far_first(frames):
         peer, source = lax.rem(f + k, frames), lax.rem(f - k + frames, frames)
         out = remote(send2.at[peer], recv2.at[f], send_sem2.at[k], recv_sem2.at[k], 0, k)
         out.start()
@@ -382,17 +419,19 @@
     want = lax.broadcasted_iota(jnp.int32, (total, slots), 1).astype(F32) + 1.0
     land = jnp.where(arrived[:, width:].astype(F32) == want, 1.0, 0.0).astype(BF16)
     canvas = lax.dot_general(land, arrived[:, :width], (((0,), (0,)), ((), ())), preferred_element_type=F32)
-    own[2] = canvas.astype(BF16).reshape(2, 64, width)
+    block[...] = canvas.astype(BF16).reshape(2, 64, width)
     third = []
     for n, (dr, df) in enumerate(near):
         src, region = {
-            0: (own.at[2], own),
-            1: (own.at[2, :, pl.ds(32, 32)], above),
-            -1: (own.at[2, :, pl.ds(0, 32)], below),
+            0: (block, own),
+            1: (block.at[:, pl.ds(32, 32)], above),
+            -1: (block.at[:, pl.ds(0, 32)], below),
         }[dr]
         out = remote(src, region.at[2 - df], send_sem3.at[n], recv_sem3.at[n], dr, df)
         out.start()
         third.append(out)
+    keep = pltpu.make_async_copy(block, own.at[2], load_sem.at[5])
+    keep.start()
     make_lift(wlift_ref, lift_ref, 1, 1)
     loads[2].wait()
     for part in range(3):
@@ -405,10 +444,7 @@
         copy.start()
     for out in third:
         out.wait_recv()
-    for part in range(3):
-        blocks_ref[part, 0:64] = above[part].reshape(64, width)
-        blocks_ref[part, 64:192] = own[part].reshape(128, width)
-        blocks_ref[part, 192:256] = below[part].reshape(64, width)
+    keep.wait()
     for out, _ in first + second:
         out.wait_send()
     for out in third:
@@ -420,27 +456,28 @@
 def exchange(latents, tile_slot, w_in, w_lift, w_final):
     rows, frames = lax.axis_size("rows"), lax.axis_size("frames")
     width = latents.shape[1]
-    vmem, hbm = pl.BlockSpec(memory_space=pltpu.VMEM), pl.BlockSpec(memory_space=pltpu.HBM)
+    hbm = pl.BlockSpec(memory_space=pltpu.HBM)
     weights = (w_in, w_lift.swapaxes(2, 3), w_final)
     made = [(768, 768), (1536, 768), (4, 768, 512)]
+    blocks = [(3, 2, 32, width), (3, 2, 64, width), (3, 2, 32, width)]
     dma = pltpu.SemaphoreType.DMA
     return pl.pallas_call(
         functools.partial(exchange_kernel, rows, frames),
-        in_specs=[vmem, vmem, hbm, hbm, hbm],
-        out_specs=[vmem, hbm, hbm, hbm],
-        out_shape=[jax.ShapeDtypeStruct(shape, BF16) for shape in [(3, 256, width)] + made],
+        in_specs=[hbm] * 5,
+        out_specs=[hbm] * 6,
+        out_shape=[jax.ShapeDtypeStruct(shape, BF16) for shape in blocks + made],
         scratch_shapes=[
+            pltpu.VMEM(latents.shape, BF16),
+            pltpu.VMEM(tile_slot.shape, jnp.int32),
             pltpu.VMEM((rows, 2 * frames, 2 * width), BF16),
             pltpu.VMEM((rows, 2 * frames, 2 * width), BF16),
             pltpu.VMEM((frames, 2 * rows, 2 * width), BF16),
             pltpu.VMEM((frames, 2 * rows, 2 * width), BF16),
-            pltpu.VMEM((3, 2, 32, width), BF16),
-            pltpu.VMEM((3, 2, 64, width), BF16),
-            pltpu.VMEM((3, 2, 32, width), BF16),
+            pltpu.VMEM((2, 64, width), BF16),
         ]
         + [pltpu.VMEM(w.shape, BF16) for w in weights]
         + [pltpu.VMEM(shape, BF16) for shape in made]
-        + [dma((3,)), dma((3,)), dma((rows,)), dma((rows,)), dma((frames,)), dma((frames,)), dma((8,)), dma((8,))],
+        + [dma((6,)), dma((3,)), dma((rows,)), dma((rows,)), dma((frames,)), dma((frames,)), dma((8,)), dma((8,))],
         compiler_params=pltpu.CompilerParams(
             collective_id=0, has_side_effects=True, vmem_limit_bytes=VMEM_LIMIT
         ),
@@ -451,8 +488,8 @@
 def shards(
     latents, tile_slot, w_in, b_in, gain_in, w_time, b_time, w_lift, b_lift, gain_lift, w_final, b_final
 ):
-    blocks, band, wl, wf = exchange(latents, tile_slot, w_in, w_lift, w_final)
-    return decode(blocks, band, wl, wf, b_in, gain_in, w_time, b_time, b_lift, gain_lift, b_final)
+    above, own, below, band, wl, wf = exchange(latents, tile_slot, w_in, w_lift, w_final)
+    return decode(above, own, below, band, wl, wf, b_in, gain_in, w_time, b_time, b_lift, gain_lift, b_final)
 
 
 def solution(mesh):

time: 64.2 us -> 61 us (0.950)
  Pallas kernels: 64 us -> 60.6 us
    pallas_call x1, Pallas kernels: 37 us -> 35.2 us  [decode(): pl.pallas_call(decode_kernel, grid=(width // XB,), in_specs=[vmem, vmem,...]
    pallas_call x1, Pallas kernels: 26.9 us -> 25.5 us  [exchange(): pl.pallas_call(functools.partial(exchange_kernel, rows, frames), in_specs...]
where the time goes in v3:
time: 61 us; the launch traced here: 60.8 us
  Pallas kernels  60.6 us (99%)
    pallas_call x1, Pallas kernels, decode(): pl.pallas_call(decode_kernel, grid=(width // XB,), in_specs=[vmem, vmem,...  35.2 us
    pallas_call x1, Pallas kernels, exchange(): pl.pallas_call(functools.partial(exchange_kernel, rows, frames), in_specs...  25.5 us

profile of v3, /device:TPU:1, one launch (start us, length us, event | category | flops | bytes accessed | tf_op | source)
XLA Modules:
  0.0 60.8 jit_solution(14581337335060762749)
XLA Ops:
  0.0 25.5 %exchange.1 = (bf16[3,2,32,128]{3,2,1,0:T(8,128)(2,1)}, bf16[3,2,64,128]{3,2,1,0:T(8,128)(2,1)}, bf16[3,2,32,128]{3,2,1,0:T(8,128)(2,1)}, bf16[768,768]{1,0:T(8,...) custom-call(bf16[128,128]{1,0:T(8,128)(2,1)} %lat_hbm.1, s32[128]{0:T(128)} %slot_hbm.1, ...), custom_call_target="tpu_custom_call" | custom-call | tf_op jit(solution)/shard_map/exchange/pallas_call | solution.py:464
  25.5 35.2 %decode.1 = bf16[4,16,49152]{2,1,0:T(8,128)(2,1)} custom-call(bf16[3,2,32,128]{3,2,1,0:T(8,128)(2,1)} %get-tuple-element.11.above_ref, bf16[3,2,64,128]{3,2,1,0:T(8,128)(2,1)} %get-tuple-element.12.own_ref, bf16[3,2,32,128]{3,2,1,0:T(8,128)(2,1)} %get-tuple-element.13.below_ref, bf16[768,768]{1,0:T(8,128)(2,1)} %get-tuple-element.14.band_hbm, f32[384]{0:T(512)} %bin_ref.1, ...), custom_call_target="tpu_custom_call" | custom-call | tf_op jit(solution)/shard_map/decode/pallas_call | solution.py:303

commit v4 on v3

--- a/solution.py
+++ b/solution.py
@@ -9,6 +9,7 @@
 
 BF16, F32 = jnp.bfloat16, jnp.float32
 XB = 64
+NCH = 3
 SUB = 32
 SC = 8
 VMEM_LIMIT = 60 * 1024 * 1024
@@ -81,6 +82,14 @@
                         for n, tile in enumerate(tiles):
                             lane = 256 * qy + 128 * n
                             final_ref[2 * jpar + xpar, slot : slot + 64, lane : lane + 128] = tile.astype(BF16)
+
+
+def weave(*lists):
+    order = sorted(
+        ((n + 0.5) / len(steps), which, n) for which, steps in enumerate(lists) for n in range(len(steps))
+    )
+    for _, which, n in order:
+        lists[which][n]()
 
 
 def front(block_refs, band_ref, bin_ref, gin_ref, wtime_ref, btime_ref, grid_ref, dbl_ref, loads):
@@ -118,13 +127,12 @@
     b_in, g_in, b_time = (v[...].reshape(1, -1) for v in (bin_ref, gin_ref, btime_ref))
     g_in = 0.5 * g_in
 
-    def chunk(step, carry):
-        s0 = step * SC
-        cells = grid_ref[:, pl.ds(s0, SC + 2)]
-        flat = cells.reshape(6 * (SC + 2), 8, 128)
-        turned = [flat, pltpu.roll(flat, 7, 1), pltpu.roll(flat, 6, 1)]
-        pieces = []
-        for q in range(4):
+    def chunk(s0):
+        pieces, hidden, feats, hist = [], [], [], []
+
+        def build(q):
+            flat = grid_ref[:, s0 : s0 + SC + 2].reshape(6 * (SC + 2), 8, 128)
+            turned = [flat, pltpu.roll(flat, 7, 1), pltpu.roll(flat, 6, 1)]
             shift = (16 - 32 * q) % 128
             parts = []
             for d, lanes in enumerate((shift, shift + 64, shift)):
@@ -138,30 +146,57 @@
                 parts.append(own)
             first = jnp.where(lane < 64, parts[0], parts[1])
             pieces.append(jnp.concatenate([first, parts[2]], axis=-1))
-        patch = jnp.stack(pieces, axis=2).reshape(6, SC * 4 * 8, 256).astype(BF16)
-        patch = jnp.concatenate([patch[k : k + 4] for k in range(3)], axis=-1)
-        hidden = jnp.dot(patch.reshape(4 * SC * 32, 768), band_ref[...], preferred_element_type=F32)
-        halves = []
-        for pp in range(2):
-            h = hidden[:, 384 * pp : 384 * (pp + 1)] + b_in
-            mean = jnp.sum(h * h, axis=-1, keepdims=True) * (1.0 / 384)
-            v = silu_of_half(h * lax.rsqrt(mean + 1e-6) * g_in)
-            halves.append(v.reshape(4, SC * 4, 8, 384))
-        feats = jnp.stack(halves, axis=2)
-        feats = jnp.concatenate([jnp.where(frame > 0, feats[:2], 0.0), feats[2:]], axis=0)
-        feats = feats.reshape(4, SC * 64, 384).astype(BF16)
-        hist = jnp.concatenate([feats[k : k + 2] for k in range(3)], axis=-1)
-        acc = jnp.dot(hist.reshape(2 * SC * 64, 1152), wtime_ref[...], preferred_element_type=F32)
-        acc = acc + b_time
-        acc = acc.reshape(2, SC * 8, 8, 768)
-        for t in range(2):
-            for j in range(2):
+
+        def gather():
+            patch = jnp.stack(pieces, axis=2).reshape(6, SC * 4 * 8, 256).astype(BF16)
+            patch = jnp.concatenate([patch[k : k + 4] for k in range(3)], axis=-1)
+            pieces.append(patch.reshape(4 * SC * 32, 768))
+
+        def expand(n):
+            out = jnp.dot(pieces[-1], band_ref[:, 256 * n : 256 * (n + 1)], preferred_element_type=F32)
+            hidden.append(out.reshape(4, SC * 32, 256))
+
+        def norm(t):
+            tiles = []
+            for pp in range(2):
+                h = []
                 for k in range(3):
-                    lanes = acc[t, :, :, 384 * j + 128 * k : 384 * j + 128 * (k + 1)]
-                    dbl_ref[k, pl.ds(8 * s0 + 1, SC * 8), pl.ds(2 * j + t, 8, stride=4), :] = lanes
-        return carry
-
-    lax.fori_loop(0, 16 // SC, chunk, 0)
+                    n = 3 * pp + k
+                    lanes = slice(128 * (n % 2), 128 * (n % 2) + 128)
+                    h.append(hidden[n // 2][t][:, lanes] + b_in[:, 128 * k : 128 * (k + 1)])
+                mean = jnp.sum(h[0] * h[0] + h[1] * h[1] + h[2] * h[2], axis=-1, keepdims=True) * (1.0 / 384)
+                factor = lax.rsqrt(mean + 1e-6)
+                tiles.append([silu_of_half(h[k] * factor * g_in[:, 128 * k : 128 * (k + 1)]) for k in range(3)])
+            merged = []
+            for k in range(3):
+                v = jnp.stack([tiles[pp][k].reshape(SC * 4, 8, 128) for pp in range(2)], axis=1)
+                if t < 2:
+                    v = jnp.where(frame > 0, v, 0.0)
+                merged.append(v.reshape(SC * 64, 128).astype(BF16))
+            feats.append(merged)
+
+        def align():
+            rows = [jnp.concatenate([v for k in range(3) for v in feats[t + k]], axis=-1) for t in range(2)]
+            hist.append(jnp.concatenate(rows, axis=0))
+
+        def double(n):
+            acc = jnp.dot(hist[0], wtime_ref[:, 256 * n : 256 * (n + 1)], preferred_element_type=F32)
+            acc = (acc + b_time[:, 256 * n : 256 * (n + 1)]).reshape(2, SC * 8, 8, 256)
+            for i in range(2):
+                j, k = (2 * n + i) // 3, (2 * n + i) % 3
+                for t in range(2):
+                    lanes = acc[t, :, :, 128 * i : 128 * (i + 1)]
+                    dbl_ref[k, 8 * s0 + 1 : 8 * (s0 + SC) + 1, pl.ds(2 * j + t, 8, stride=4), :] = lanes
+
+        return (
+            [functools.partial(build, q) for q in range(4)] + [gather] + [functools.partial(expand, n) for n in range(3)],
+            [functools.partial(norm, t) for t in range(4)],
+            [align] + [functools.partial(double, n) for n in range(3)],
+        )
+
+    chunks = [chunk(s0) for s0 in range(0, 16, SC)]
+    for turn in range(len(chunks) + 2):
+        weave(*(chunks[turn - n][n] for n in range(3) if 0 <= turn - n < len(chunks)))
 
     @pl.when(top)
     def _():
@@ -172,95 +207,145 @@
         dbl_ref[:, :, 20:24, :] = jnp.zeros((3, dbl_ref.shape[1], 4, 128), F32)
 
 
-def back(step, sub, dbl_ref, wl_ref, bl_ref, gl_ref, wf_ref, bf_ref, out_ref, rows_ref, sec_ref):
-    row = lax.axis_index("rows")
-    top, bottom = row == 0, row == lax.axis_size("rows") - 1
-    width = dbl_ref.shape[1] - 2
-    x0 = step * XB + sub
-    count = SUB + 1
-    lane = lax.broadcasted_iota(jnp.int32, (1, 1, 128), 2)
-    low = lane < 64
-    half = lax.broadcasted_iota(jnp.int32, (1, 8, 1), 1) < 4
-
-    patch = []
-    for ty in range(2):
-        tiles = [dbl_ref[k, pl.ds(x0, count + 1), 4 * ty : 4 * ty + 24, :] for k in range(3)]
-        patch += [v[tx : tx + count].reshape(count * 24, 128).astype(BF16) for tx in range(2) for v in tiles]
-    acc = jnp.dot(jnp.concatenate(patch, axis=-1), wl_ref[...], preferred_element_type=F32)
-    acc = acc.reshape(count, 24, 768) + bl_ref[...]
-    first_rows = lax.broadcasted_iota(jnp.int32, (1, 8, 1), 1) < 4
-    above, below = jnp.logical_and(first_rows, top), jnp.logical_and(first_rows, bottom)
-
-    def keep(n, v):
+class Columns:
+    def __init__(self, step, sub, dbl_ref, wl_ref, bl_ref, gl_ref, wf_ref, bf_ref, out_ref, rows_ref, sec_ref):
+        row = lax.axis_index("rows")
+        self.top, self.bottom = row == 0, row == lax.axis_size("rows") - 1
+        self.width = dbl_ref.shape[1] - 2
+        self.x0, self.sub, self.count = step * XB + sub, sub, SUB + 1
+        self.low = lax.broadcasted_iota(jnp.int32, (1, 1, 128), 2) < 64
+        self.lane = lax.broadcasted_iota(jnp.int32, (1, 1, 128), 2)
+        self.half = lax.broadcasted_iota(jnp.int32, (1, 8, 1), 1) < 4
+        self.dbl_ref, self.wl_ref, self.bl_ref, self.gl_ref = dbl_ref, wl_ref, bl_ref, gl_ref
+        self.wf_ref, self.bf_ref, self.out_ref, self.rows_ref = wf_ref, bf_ref, out_ref, rows_ref
+        self.sec_ref = sec_ref.at[sub // SUB]
+        self.acc, self.results, self.s_m, self.s_p, self.s_e = {}, {}, [], [], []
+
+    def load(self):
+        patch = []
+        for ty in range(2):
+            tiles = [self.dbl_ref[k, pl.ds(self.x0, self.count + 1), 4 * ty : 4 * ty + 24, :] for k in range(3)]
+            patch += [
+                v[tx : tx + self.count].reshape(self.count * 24, 128).astype(BF16) for tx in range(2) for v in tiles
+            ]
+        self.patch = jnp.concatenate(patch, axis=-1)
+
+    def lift_steps(self):
+        def part(n):
+            w = self.wl_ref[:, 256 * n : 256 * (n + 1)]
+            acc = jnp.dot(self.patch, w, preferred_element_type=F32)
+            self.acc[n] = acc.reshape(self.count, 24, 256)
+
+        return [self.load] + [functools.partial(part, n) for n in range(3)]
+
+    def keep(self, n, lo, hi, v):
         px, k = n // 3, n % 3
+        first_rows = lax.broadcasted_iota(jnp.int32, (1, 8, 1), 1) < 4
+        above, below = jnp.logical_and(first_rows, self.top), jnp.logical_and(first_rows, self.bottom)
         for g in range(3):
             part = v[:, 8 * g : 8 * (g + 1)]
             if g == 0 and k < 2:
-                part = jnp.where(above if k == 0 else jnp.logical_and(above, low), 0.0, part)
+                part = jnp.where(above if k == 0 else jnp.logical_and(above, self.low), 0.0, part)
             if g == 2 and k > 0:
-                part = jnp.where(below if k == 2 else jnp.logical_and(below, jnp.logical_not(low)), 0.0, part)
+                part = jnp.where(below if k == 2 else jnp.logical_and(below, jnp.logical_not(self.low)), 0.0, part)
             rows = slice(16 + 8 * g, 24 + 8 * g)
-            if px == 0:
-                sec_ref[sub // SUB, n, 0:1, rows, :] = jnp.where(x0 == 0, 0.0, part[0:1])
-                sec_ref[sub // SUB, n, 1:count, rows, :] = part[1:]
+            if px == 0 and lo == 0:
+                self.sec_ref[n, 0:1, rows, :] = jnp.where(self.x0 == 0, 0.0, part[0:1])
+                self.sec_ref[n, 1:hi, rows, :] = part[1:]
+            elif px == 1 and hi == self.count:
+                self.sec_ref[n, lo : hi - 1, rows, :] = part[:-1]
+                self.sec_ref[n, hi - 1 : hi, rows, :] = jnp.where(self.x0 == self.width - SUB, 0.0, part[-1:])
             else:
-                sec_ref[sub // SUB, n, 0 : count - 1, rows, :] = part[:-1]
-                sec_ref[sub // SUB, n, count - 1 : count, rows, :] = jnp.where(x0 == width - SUB, 0.0, part[-1:])
-
-    for px in range(2):
-        tiles = [acc[..., 384 * px + 128 * k : 384 * px + 128 * (k + 1)] for k in range(3)]
-        sq = [v * v for v in tiles]
-        s0 = jnp.sum(sq[0] + jnp.where(low, sq[1], 0.0), axis=-1, keepdims=True)
-        s1 = jnp.sum(sq[2] + jnp.where(low, 0.0, sq[1]), axis=-1, keepdims=True)
-        f0 = lax.rsqrt(s0 * (1.0 / 192) + 1e-6)
-        f1 = lax.rsqrt(s1 * (1.0 / 192) + 1e-6)
-        for k, f in enumerate((f0, jnp.where(low, f0, f1), f1)):
-            v = silu_of_half(tiles[k] * f * gl_ref[:, 384 * px + 128 * k : 384 * px + 128 * (k + 1)])
-            keep(3 * px + k, v)
-
-    def window(k, first):
+                self.sec_ref[n, lo:hi, rows, :] = part
+
+    def norm_steps(self):
+        def part(lo, hi, px):
+            tiles = []
+            for k in range(3):
+                n = 3 * px + k
+                lanes = slice(128 * (n % 2), 128 * (n % 2) + 128)
+                tiles.append(self.acc[n // 2][lo:hi, :, lanes] + self.bl_ref[:, 128 * n : 128 * (n + 1)])
+            sq = [v * v for v in tiles]
+            s0 = jnp.sum(sq[0] + jnp.where(self.low, sq[1], 0.0), axis=-1, keepdims=True)
+            s1 = jnp.sum(sq[2] + jnp.where(self.low, 0.0, sq[1]), axis=-1, keepdims=True)
+            f0 = lax.rsqrt(s0 * (1.0 / 192) + 1e-6)
+            f1 = lax.rsqrt(s1 * (1.0 / 192) + 1e-6)
+            for k, f in enumerate((f0, jnp.where(self.low, f0, f1), f1)):
+                n = 3 * px + k
+                v = silu_of_half(tiles[k] * f * self.gl_ref[:, 128 * n : 128 * (n + 1)])
+                self.keep(n, lo, hi, v)
+
+        cuts = [self.count * c // NCH for c in range(NCH + 1)]
+        return [functools.partial(part, lo, hi, px) for px in range(2) for lo, hi in zip(cuts, cuts[1:])]
+
+    def window(self, k, first):
         out = []
         for h in range(2):
-            lo = sec_ref[sub // SUB, k, :, pl.ds(16 + 4 * first + 2 * h, 8, stride=4), :]
-            hi = sec_ref[sub // SUB, k, :, pl.ds(4 * first + 2 * h + 1, 8, stride=4), :]
-            out.append(jnp.where(half, lo, hi))
+            lo = self.sec_ref[k, :, pl.ds(16 + 4 * first + 2 * h, 8, stride=4), :]
+            hi = self.sec_ref[k, :, pl.ds(4 * first + 2 * h + 1, 8, stride=4), :]
+            out.append(jnp.where(self.half, lo, hi))
         return jnp.concatenate(out, axis=1).astype(BF16)
 
-    s_m = [window(k, 0) for k in range(6)]
-    s_p = [window(k, 1) for k in range(6)]
-    s_e = []
-    for px in range(2):
-        s_e += [s_p[3 * px], jnp.where(low, s_p[3 * px + 1], s_m[3 * px + 1]), s_m[3 * px + 2]]
-
-    def odd(tiles):
-        return jnp.concatenate(tiles, axis=-1).reshape(count * 16, 768)
-
-    def even(tiles):
-        return jnp.concatenate([v[1:] for v in tiles[:3]] + [v[:-1] for v in tiles[3:]], axis=-1).reshape(SUB * 16, 768)
-
-    def mul(lhs, kind, lo, hi):
-        return jnp.dot(lhs, wf_ref[kind, :, lo:hi], preferred_element_type=F32).reshape(-1, 16, hi - lo)
-
-    e_o, e_e = mul(odd(s_e), 1, 0, 512), mul(even(s_e), 0, 0, 512)
-    results = (
-        (mul(odd(s_m), 3, 256, 512), mul(even(s_m), 2, 256, 512)),
-        (e_o[..., :256], e_e[..., :256]),
-        (e_o[..., 256:], e_e[..., 256:]),
-        (mul(odd(s_p), 3, 0, 256), mul(even(s_p), 2, 0, 256)),
-    )
-    for a, (o, e) in enumerate(results):
-        t0 = jnp.where(lane < 96, o[:-1, :, 128:], e[..., :128])
+    def final_steps(self):
+        def windows():
+            self.s_m = [self.window(k, 0) for k in range(6)]
+            self.s_p = [self.window(k, 1) for k in range(6)]
+            for px in range(2):
+                mixed = jnp.where(self.low, self.s_p[3 * px + 1], self.s_m[3 * px + 1])
+                self.s_e += [self.s_p[3 * px], mixed, self.s_m[3 * px + 2]]
+
+        def mul(a, source, kind, lo, even):
+            tiles = getattr(self, source)
+            if even:
+                tiles = [v[1:] for v in tiles[:3]] + [v[:-1] for v in tiles[3:]]
+            lhs = jnp.concatenate(tiles, axis=-1).reshape(-1, 768)
+            w = self.wf_ref[kind, :, lo : lo + 256]
+            self.results[a, even] = jnp.dot(lhs, w, preferred_element_type=F32).reshape(-1, 16, 256)
+
+        plan = ((1, "s_e", 1, 0), (2, "s_e", 1, 256), (0, "s_m", 3, 256), (3, "s_p", 3, 0))
+        steps = [windows]
+        for a, source, kind, lo in plan:
+            steps += [
+                functools.partial(mul, a, source, kind, lo, False),
+                functools.partial(mul, a, source, kind - 1, lo, True),
+                functools.partial(self.place, a),
+            ]
+        return steps
+
+    def place(self, a):
+        o, e = self.results[a, False], self.results[a, True]
+        t0 = jnp.where(self.lane < 96, o[:-1, :, 128:], e[..., :128])
         t1 = e[..., 128:]
-        t2 = jnp.where(lane < 32, e[..., :128], o[1:, :, :128])
+        t2 = jnp.where(self.lane < 32, e[..., :128], o[1:, :, :128])
         for k, t in enumerate((t0, t1, t2)):
-            t = t + bf_ref[:, 128 * k : 128 * (k + 1)]
+            t = t + self.bf_ref[:, 128 * k : 128 * (k + 1)]
             for u in range(SUB):
-                rows_ref[3 * (sub + u) + k, pl.ds(a, 16, stride=4), :] = t[u]
-    for j in range(2):
-        for t in range(2):
+                self.rows_ref[3 * (self.sub + u) + k, pl.ds(a, 16, stride=4), :] = t[u]
+
+    def store_steps(self):
+        def part(j, t):
             base = 16 * (2 * j + t)
-            for n in range(3 * sub, 3 * (sub + SUB)):
-                out_ref[2 * t + j, :, 128 * n : 128 * (n + 1)] = rows_ref[n, base : base + 16, :].astype(BF16)
+            for n in range(3 * self.sub, 3 * (self.sub + SUB)):
+                rows = self.rows_ref[n, base : base + 16, :]
+                self.out_ref[2 * t + j, :, 128 * n : 128 * (n + 1)] = rows.astype(BF16)
+
+        return [functools.partial(part, j, t) for j in range(2) for t in range(2)]
+
+
+def back(step, *refs):
+    parts = [Columns(step, sub, *refs) for sub in range(0, XB, SUB)]
+    last = len(parts) - 1
+    for turn in range(len(parts) + 3):
+        lists = []
+        if turn <= last:
+            lists.append(parts[turn].lift_steps())
+        if 0 <= turn - 1 <= last:
+            lists.append(parts[turn - 1].norm_steps())
+        if 0 <= turn - 2 <= last:
+            lists.append(parts[turn - 2].final_steps())
+        if 0 <= turn - 3 <= last:
+            lists.append(parts[turn - 3].store_steps())
+        weave(*lists)
 
 
 def spread(half):
@@ -291,8 +376,7 @@
         loads[2].wait()
         loads[3].wait()
 
-    for sub in range(0, XB, SUB):
-        back(step, sub, dbl_ref, wl_ref, bl_ref, gl_ref, wf_ref, bf_ref, out_ref, rows_ref, sec_ref)
+    back(step, dbl_ref, wl_ref, bl_ref, gl_ref, wf_ref, bf_ref, out_ref, rows_ref, sec_ref)
 
 
 def decode(above, own, below, band, wl, wf, b_in, gain_in, w_time, b_time, b_lift, gain_lift, b_final):

time: 61 us -> 55 us (0.902)
  Pallas kernels: 60.6 us -> 54.7 us
    pallas_call x1, Pallas kernels: 35.2 us -> 29.2 us  [decode(): pl.pallas_call(decode_kernel, grid=(width // XB,), in_specs=[vmem, vmem,...]
where the time goes in v4:
time: 55 us; the launch traced here: 54.8 us
  Pallas kernels  54.7 us (99%)
    pallas_call x1, Pallas kernels, decode(): pl.pallas_call(decode_kernel, grid=(width // XB,), in_specs=[vmem, vmem,...  29.2 us
    pallas_call x1, Pallas kernels, exchange(): pl.pallas_call(functools.partial(exchange_kernel, rows, frames), in_specs...  25.5 us

profile of v4, /device:TPU:1, one launch (start us, length us, event | category | flops | bytes accessed | tf_op | source)
XLA Modules:
  0.0 54.8 jit_solution(1853963616400111818)
XLA Ops:
  0.0 25.5 %exchange.1 = (bf16[3,2,32,128]{3,2,1,0:T(8,128)(2,1)}, bf16[3,2,64,128]{3,2,1,0:T(8,128)(2,1)}, bf16[3,2,32,128]{3,2,1,0:T(8,128)(2,1)}, bf16[768,768]{1,0:T(8,...) custom-call(bf16[128,128]{1,0:T(8,128)(2,1)} %lat_hbm.1, s32[128]{0:T(128)} %slot_hbm.1, ...), custom_call_target="tpu_custom_call" | custom-call | tf_op jit(solution)/shard_map/exchange/pallas_call | solution.py:548
  25.5 29.2 %decode.1 = bf16[4,16,49152]{2,1,0:T(8,128)(2,1)} custom-call(bf16[3,2,32,128]{3,2,1,0:T(8,128)(2,1)} %get-tuple-element.11.above_ref, bf16[3,2,64,128]{3,2,1,0:T(8,128)(2,1)} %get-tuple-element.12.own_ref, bf16[3,2,32,128]{3,2,1,0:T(8,128)(2,1)} %get-tuple-element.13.below_ref, bf16[768,768]{1,0:T(8,128)(2,1)} %get-tuple-element.14.band_hbm, f32[384]{0:T(512)} %bin_ref.1, ...), custom_call_target="tpu_custom_call" | custom-call | tf_op jit(solution)/shard_map/decode/pallas_call | solution.py:387

commit v5 on v4

--- a/solution.py
+++ b/solution.py
@@ -92,7 +92,7 @@
         lists[which][n]()
 
 
-def front(block_refs, band_ref, bin_ref, gin_ref, wtime_ref, btime_ref, grid_ref, dbl_ref, loads):
+def front(block_refs, band_ref, bin_ref, gin_ref, wtime_ref, btime_ref, grid_ref, dbl_ref, waits):
     row, frame = lax.axis_index("rows"), lax.axis_index("frames")
     top, bottom = row == 0, row == lax.axis_size("rows") - 1
     out_row = lax.broadcasted_iota(jnp.int32, (256, 256), 0)
@@ -122,8 +122,6 @@
     dbl_ref[:, 0:1] = edge_col
     dbl_ref[:, dbl_ref.shape[1] - 1 :] = edge_col
 
-    loads[0].wait()
-    loads[1].wait()
     b_in, g_in, b_time = (v[...].reshape(1, -1) for v in (bin_ref, gin_ref, btime_ref))
     g_in = 0.5 * g_in
 
@@ -196,6 +194,8 @@
 
     chunks = [chunk(s0) for s0 in range(0, 16, SC)]
     for turn in range(len(chunks) + 2):
+        if turn in waits:
+            waits[turn].wait()
         weave(*(chunks[turn - n][n] for n in range(3) if 0 <= turn - n < len(chunks)))
 
     @pl.when(top)
@@ -353,55 +353,56 @@
     return jnp.concatenate([wide, narrow, narrow, wide] * 2, axis=-1)
 
 
-def decode_kernel(
-    above_ref, own_ref, below_ref, band_hbm, bin_ref, gin_ref, wtime_hbm, btime_ref, lift_hbm, blift_ref, glift_ref, final_hbm, bfinal_ref,
-    out_ref, grid_ref, dbl_ref, rows_ref, sec_ref, band_ref, wtime_ref, wl_ref, wf_ref, bl_ref, gl_ref, bf_ref, load_sem,
-):
+def decode_kernel(count, *refs):
+    sources, out_ref, copies = refs[:count], refs[count], refs[count + 1 : 2 * count + 1]
+    grid_ref, dbl_ref, rows_ref, sec_ref, bl_ref, gl_ref, bf_ref, load_sem = refs[2 * count + 1 :]
+    blocks, (bin_ref, gin_ref, btime_ref, blift_ref, glift_ref, bfinal_ref) = copies[:3], copies[3:9]
+    band_ref, wtime_ref, wl_ref, wf_ref = copies[9:]
     step = pl.program_id(0)
 
     @pl.when(step == 0)
     def _():
-        loads = [
-            pltpu.make_async_copy(src, dst, load_sem.at[n])
-            for n, (src, dst) in enumerate(
-                ((band_hbm, band_ref), (wtime_hbm, wtime_ref), (lift_hbm, wl_ref), (final_hbm, wf_ref))
-            )
-        ]
+        loads = [pltpu.make_async_copy(src, dst, load_sem.at[n]) for n, (src, dst) in enumerate(zip(sources, copies))]
         for copy in loads:
             copy.start()
+        for copy in loads[:9]:
+            copy.wait()
         bl_ref[...] = spread(blift_ref[...].reshape(1, -1))
         gl_ref[...] = 0.5 * spread(glift_ref[...].reshape(1, -1))
         bf_ref[...] = jnp.concatenate([bfinal_ref[...].reshape(1, -1)] * 4, axis=-1)
-        front((above_ref, own_ref, below_ref), band_ref, bin_ref, gin_ref, wtime_ref, btime_ref, grid_ref, dbl_ref, loads)
-        loads[2].wait()
-        loads[3].wait()
+        waits = {0: loads[9], 2: loads[10]}
+        front(blocks, band_ref, bin_ref, gin_ref, wtime_ref, btime_ref, grid_ref, dbl_ref, waits)
+        loads[11].wait()
+        loads[12].wait()
 
     back(step, dbl_ref, wl_ref, bl_ref, gl_ref, wf_ref, bf_ref, out_ref, rows_ref, sec_ref)
 
 
 def decode(above, own, below, band, wl, wf, b_in, gain_in, w_time, b_time, b_lift, gain_lift, b_final):
     width = 128
-    vmem, hbm = pl.BlockSpec(memory_space=pltpu.VMEM), pl.BlockSpec(memory_space=pltpu.HBM)
+    hbm = pl.BlockSpec(memory_space=pltpu.HBM)
     w_time = w_time.reshape(-1, w_time.shape[-1])
-    weights = (band, w_time, wl, wf)
+    args = (above, own, below, b_in, gain_in, b_time, b_lift, gain_lift, b_final, band, w_time, wl, wf)
     return pl.pallas_call(
-        decode_kernel,
+        functools.partial(decode_kernel, len(args)),
         grid=(width // XB,),
-        in_specs=[vmem, vmem, vmem, hbm, vmem, vmem, hbm, vmem, hbm, vmem, vmem, hbm, vmem],
+        in_specs=[hbm] * len(args),
         out_specs=pl.BlockSpec((4, 16, XB * 384), lambda i: (0, 0, i)),
         out_shape=jax.ShapeDtypeStruct((4, 16, width * 384), BF16),
-        scratch_shapes=[
+        scratch_shapes=[pltpu.VMEM(v.shape, v.dtype) for v in args]
+        + [
             pltpu.VMEM((6, 18, 8, 128), F32),
             pltpu.VMEM((3, width + 2, 32, 128), F32),
             pltpu.VMEM((XB * 3, 64, 128), F32),
             pltpu.VMEM((XB // SUB, 6, SUB + 1, 56, 128), F32),
-        ]
-        + [pltpu.VMEM(w.shape, BF16) for w in weights]
-        + [pltpu.VMEM((1, 768), F32), pltpu.VMEM((1, 768), F32), pltpu.VMEM((1, 384), F32)]
-        + [pltpu.SemaphoreType.DMA((4,))],
+            pltpu.VMEM((1, 768), F32),
+            pltpu.VMEM((1, 768), F32),
+            pltpu.VMEM((1, 384), F32),
+            pltpu.SemaphoreType.DMA((len(args),)),
+        ],
         compiler_params=pltpu.CompilerParams(vmem_limit_bytes=VMEM_LIMIT),
         name="decode",
-    )(above, own, below, band, b_in, gain_in, w_time, b_time, wl, b_lift, gain_lift, wf, b_final)
+    )(*args)
 
 
 def far_first(count):

time: 55 us -> 54.1 us (0.984)
  Pallas kernels: 54.7 us -> 53.8 us
    pallas_call x1, Pallas kernels: 29.2 us -> 28.4 us  [decode(): pl.pallas_call(functools.partial(decode_kernel, len(args)), grid=(width /...]
where the time goes in v5:
time: 54.1 us; the launch traced here: 54 us
  Pallas kernels  53.8 us (99%)
    pallas_call x1, Pallas kernels, decode(): pl.pallas_call(functools.partial(decode_kernel, len(args)), grid=(width /...  28.4 us
    pallas_call x1, Pallas kernels, exchange(): pl.pallas_call(functools.partial(exchange_kernel, rows, frames), in_specs...  25.5 us

profile of v5, /device:TPU:1, one launch (start us, length us, event | category | flops | bytes accessed | tf_op | source)
XLA Modules:
  0.0 54.0 jit_solution(13056512493084476727)
XLA Ops:
  0.0 25.5 %exchange.1 = (bf16[3,2,32,128]{3,2,1,0:T(8,128)(2,1)}, bf16[3,2,64,128]{3,2,1,0:T(8,128)(2,1)}, bf16[3,2,32,128]{3,2,1,0:T(8,128)(2,1)}, bf16[768,768]{1,0:T(8,...) custom-call(bf16[128,128]{1,0:T(8,128)(2,1)} %lat_hbm.1, s32[128]{0:T(128)} %slot_hbm.1, ...), custom_call_target="tpu_custom_call" | custom-call | tf_op jit(solution)/shard_map/exchange/pallas_call | solution.py:549
  25.5 28.4 %decode.1 = bf16[4,16,49152]{2,1,0:T(8,128)(2,1)} custom-call(bf16[3,2,32,128]{3,2,1,0:T(8,128)(2,1)} %get-tuple-element.11.refs_0_, bf16[3,2,64,128]{3,2,1,0:T(8,128)(2,1)} %get-tuple-element.12.refs_1_, bf16[3,2,32,128]{3,2,1,0:T(8,128)(2,1)} %get-tuple-element.13.refs_2_, f32[384]{0:T(512)} %refs_3_.1, f32[384]{0:T(512)} %refs_4_.1, f32[768]{0:T(1024)} %refs_5_.1, ...), custom_call_target="tpu_custom_call" | custom-call | tf_op jit(solution)/shard_map/decode/pallas_call | solution.py:386

commit v6 on v5

--- a/solution.py
+++ b/solution.py
@@ -432,10 +432,10 @@
     def at(dr, df):
         return {"rows": lax.rem(r + dr + rows, rows), "frames": lax.rem(f + df + frames, frames)}
 
-    near = [(dr, df) for df in range(3) for dr in (0, 1, -1) if (dr, df) != (0, 0)]
+    near = [(dr, df) for df in (2, 1, 0) for dr in (1, -1, 0) if (dr, df) != (0, 0)]
     far = [(dr, df) for dr, df in near if dr != 0 and df != 0]
     barrier = pltpu.get_barrier_semaphore()
-    sources = [(k, 0) for k in range(1, rows)] + [(0, k) for k in range(1, frames)] + [(-dr, -df) for dr, df in far]
+    sources = [(-dr, -df) for dr, df in far] + [(0, k) for k in far_first(frames)] + [(k, 0) for k in far_first(rows)]
     for dr, df in sources:
         pl.semaphore_signal(barrier, inc=1, device_id=at(dr, df), device_id_type=pl.DeviceIdType.MESH)
 

time: 54.1 us -> 53.4 us (0.987); the launches traced: 54 us -> 52.7 us
  Pallas kernels: 53.8 us -> 52.5 us
    pallas_call x1, Pallas kernels: 25.5 us -> 24.2 us  [exchange(): pl.pallas_call(functools.partial(exchange_kernel, rows, frames), in_specs...]
where the time goes in v6:
time: 53.4 us; the launch traced here: 52.7 us
  Pallas kernels  52.5 us (98%)
    pallas_call x1, Pallas kernels, decode(): pl.pallas_call(functools.partial(decode_kernel, len(args)), grid=(width /...  28.4 us
    pallas_call x1, Pallas kernels, exchange(): pl.pallas_call(functools.partial(exchange_kernel, rows, frames), in_specs...  24.2 us

profile of v6, /device:TPU:1, one launch (start us, length us, event | category | flops | bytes accessed | tf_op | source)
XLA Modules:
  0.0 52.7 jit_solution(12183002980931847632)
XLA Ops:
  0.0 24.2 %exchange.1 = (bf16[3,2,32,128]{3,2,1,0:T(8,128)(2,1)}, bf16[3,2,64,128]{3,2,1,0:T(8,128)(2,1)}, bf16[3,2,32,128]{3,2,1,0:T(8,128)(2,1)}, bf16[768,768]{1,0:T(8,...) custom-call(bf16[128,128]{1,0:T(8,128)(2,1)} %lat_hbm.1, s32[128]{0:T(128)} %slot_hbm.1, ...), custom_call_target="tpu_custom_call" | custom-call | tf_op jit(solution)/shard_map/exchange/pallas_call | solution.py:549
  24.2 28.4 %decode.1 = bf16[4,16,49152]{2,1,0:T(8,128)(2,1)} custom-call(bf16[3,2,32,128]{3,2,1,0:T(8,128)(2,1)} %get-tuple-element.11.refs_0_, bf16[3,2,64,128]{3,2,1,0:T(8,128)(2,1)} %get-tuple-element.12.refs_1_, bf16[3,2,32,128]{3,2,1,0:T(8,128)(2,1)} %get-tuple-element.13.refs_2_, f32[384]{0:T(512)} %refs_3_.1, f32[384]{0:T(512)} %refs_4_.1, f32[768]{0:T(1024)} %refs_5_.1, ...), custom_call_target="tpu_custom_call" | custom-call | tf_op jit(solution)/shard_map/decode/pallas_call | solution.py:386
